TPU v7x, 512 devices: a whole 4x8x8 slice. The times are simulated.
512 devices in a mesh: gx: 32 (over z, x), gy: 16 (over y, core).
Axes of the slice: x: 4, y: 8, z: 8, core: 2. Of those that a mesh axis runs over, the one named last changes fastest.
Arguments:
- basis: float32 [32, 256, 2048], P(None, 'gx', 'gy'), may hold values from -6 to 6
- search: float32 [32, 256, 2048], P(None, 'gx', 'gy'), may hold values from -6 to 6
- conductivity: float32 [256, 2048], P('gx', 'gy'), may hold values from 0.2 to 5
- rotation: int32 [96, 32], replicated, may hold values from -4 to 4
Outputs:
- new_basis: float32 [32, 256, 2048], P(None, 'gx', 'gy')
- new_search: float32 [32, 256, 2048], P(None, 'gx', 'gy')
- ritz_values: float32 [32], replicated
All inputs are finite; a program needn't handle non-finite values.
Results may differ from a plain program's by a relative error of at most 0.0003.
Values sent between devices are 32-bit elements; how exact they have to be, the bound alone decides.
No kernel may reach another device: no remote copies, remote signals or barrier semaphores. Data moves between devices by JAX's collectives and lax.ppermute only.
A program may use at most 64 MiB of HBM per device.

v0:
```python
import jax
import jax.numpy as jnp
from jax import lax
from jax.sharding import PartitionSpec as P

CZ = 16


HIGH = lax.Precision.HIGHEST


def padded_2(block, sides, width):
    for axis, dim in sides:
        count = lax.axis_size(axis)
        forward = [(i, i + 1) for i in range(count - 1)]
        backward = [(target, source) for source, target in forward]
        low = lax.ppermute(
            lax.slice_in_dim(block, block.shape[dim] - width, None, axis=dim), axis, forward
        )
        high = lax.ppermute(lax.slice_in_dim(block, 0, width, axis=dim), axis, backward)
        block = jnp.concatenate([low, block, high], axis=dim)
    return block


def stencil(padded, cond_pad):
    fields = padded.shape[0]
    rows_x = padded.shape[1] - 2
    span = (padded.shape[2] - 2) * CZ
    flat_pad = padded.reshape(fields, rows_x + 2, padded.shape[2] * CZ)
    cond_flat = cond_pad.reshape(rows_x + 2, padded.shape[2] * CZ)
    middle = flat_pad[:, 1:-1, CZ : CZ + span]
    cond_mid = cond_flat[1:-1, CZ : CZ + span]
    total = jnp.zeros_like(middle)
    for offset_x, offset_y in ((2, CZ), (0, CZ), (1, 2 * CZ), (1, 0)):
        beside = flat_pad[:, offset_x : offset_x + rows_x, offset_y : offset_y + span]
        cond_side = cond_flat[offset_x : offset_x + rows_x, offset_y : offset_y + span]
        total = total + 0.5 * (cond_mid + cond_side) * (middle - beside)
    depth = lax.broadcasted_iota(jnp.int32, (1, span), 1) % CZ
    top_end = depth == CZ - 1
    low_end = depth == 0

    def upward(array):
        return jnp.where(top_end, jnp.roll(array, CZ - 1, -1), jnp.roll(array, -1, -1))

    def downward(array):
        return jnp.where(low_end, jnp.roll(array, 1 - CZ, -1), jnp.roll(array, 1, -1))

    for mover in (upward, downward):
        total = total + 0.5 * (cond_mid + mover(cond_mid)) * (middle - mover(middle))
    return total


def cross(left, right):
    return lax.dot_general(
        left, right, (((1,), (1,)), ((), ())), precision=HIGH, preferred_element_type=jnp.float32
    )


def chol_lower(matrix):
    size = matrix.shape[0]
    index = lax.broadcasted_iota(jnp.int32, (size,), 0)

    def column(j, lower):
        row_j = lax.dynamic_slice_in_dim(lower, j, 1, 0)[0]
        col_a = lax.dynamic_slice_in_dim(matrix, j, 1, 1)[:, 0]
        vec = col_a - jnp.dot(lower, row_j, precision=HIGH)
        pivot = jnp.sqrt(jnp.sum(jnp.where(index == j, vec, 0.0)))
        col = jnp.where(index >= j, vec / pivot, 0.0)
        return jnp.where(index[None, :] == j, col[:, None], lower)

    return lax.fori_loop(0, size, column, jnp.zeros_like(matrix))


def lower_inverse(lower):
    size = lower.shape[0]
    index = lax.broadcasted_iota(jnp.int32, (size,), 0)
    ident = jnp.eye(size, dtype=lower.dtype)

    def row(i, result):
        l_row = lax.dynamic_slice_in_dim(lower, i, 1, 0)[0]
        e_row = lax.dynamic_slice_in_dim(ident, i, 1, 0)[0]
        pivot = jnp.sum(jnp.where(index == i, l_row, 0.0))
        fresh_row = (e_row - jnp.dot(l_row, result, precision=HIGH)) / pivot
        return jnp.where(index[:, None] == i, fresh_row[None, :], result)

    return lax.fori_loop(0, size, row, jnp.zeros_like(lower))


def finish(full, gram, projected, rotation):
    modes = rotation.shape[1]
    inverse = lower_inverse(chol_lower(gram)).T
    ritz = jnp.dot(inverse.T, jnp.dot(projected, inverse, precision=HIGH), precision=HIGH)
    ritz = 0.5 * (ritz + ritz.T)
    bound = jnp.max(jnp.sum(jnp.abs(ritz), 1))
    start = rotation.astype(jnp.float32)
    moved = bound * start - jnp.dot(ritz, start, precision=HIGH)
    lower = chol_lower(jnp.dot(moved.T, moved, precision=HIGH))
    coeffs = jnp.dot(moved, lower_inverse(lower).T, precision=HIGH)
    values = jnp.sum(coeffs * jnp.dot(ritz, coeffs, precision=HIGH), 0)
    weights = jnp.dot(inverse, coeffs, precision=HIGH)
    dims = (((0,), (0,)), ((), ()))
    fresh = lax.dot_general(weights, full, dims, precision=HIGH, preferred_element_type=jnp.float32)
    directions = lax.dot_general(
        weights[modes:], full[modes:], dims, precision=HIGH, preferred_element_type=jnp.float32
    )
    return (fresh, directions, values)


def sum_pair(gram_part, proj_part):
    return lax.psum((gram_part, proj_part), ("gx", "gy"))


def body(basis, search, conductivity, rotation):
    modes, cells_x, flat = basis.shape
    cells_y = flat // CZ
    local = cells_x * flat
    count = local * lax.axis_size("gx") * lax.axis_size("gy")
    stacked = jnp.concatenate([basis, search, conductivity[None]], 0).reshape(
        2 * modes + 1, cells_x, cells_y, CZ
    )
    basis_flat = basis.reshape(modes, local)
    search_flat = search.reshape(modes, local)
    padded = padded_2(stacked, (("gx", 1), ("gy", 2)), 1)
    cond_pad = padded[-1]
    images = stencil(padded[:-1], cond_pad).reshape(2 * modes, local)
    image_x = images[:modes]
    image_p = images[modes:]
    along, norms = lax.psum(
        (jnp.sum(basis_flat * image_x, 1), jnp.sum(basis_flat * basis_flat, 1)), ("gx", "gy")
    )
    quotient = along / norms
    residual = image_x - quotient[:, None] * basis_flat
    field = image_x - quotient[:, None] * basis_flat
    padded_two = padded_2(field.reshape(modes, cells_x, cells_y, CZ), (("gx", 1), ("gy", 2)), 1)
    image_w = stencil(padded_two, cond_pad).reshape(modes, local)
    full = jnp.concatenate([basis_flat, residual, search_flat], 0)
    image_all = jnp.concatenate([image_x, image_w, image_p], 0)
    gram_sum, proj_sum = sum_pair(cross(full, full), cross(full, image_all))
    fresh, directions, values = finish(full, gram_sum / count, proj_sum / count, rotation)
    return (fresh.reshape(modes, cells_x, flat), directions.reshape(modes, cells_x, flat), values)


def solution(mesh):
    in_specs = (P(None, "gx", "gy"), P(None, "gx", "gy"), P("gx", "gy"), P())
    out_specs = (P(None, "gx", "gy"), P(None, "gx", "gy"), P())
    return jax.shard_map(body, mesh=mesh, in_specs=in_specs, out_specs=out_specs, check_vma=False)
```

profile of v0, /device:TPU:1, one launch (start us, length us, event | category | flops | bytes accessed | tf_op | source)
XLA Modules:
  0.0 838.3 jit_solution(13734582309623677147)
XLA Ops:
  7.2 1.1 copy.64
  9.6 3.9 collective-permute-start
  13.5 1.3 collective-permute-start.1
  15.2 3.3 collective-permute-done.1
  18.7 5.2 collective-permute-start.2
  23.9 3.4 collective-permute-start.3
  27.3 2.3 collective-permute-done.3
  31.3 1.2 fusion.45
  32.7 106.5 %all-reduce.1 = (f32[32]{0:T(128)S(1)}, f32[32]{0:T(128)S(1)}) all-reduce(f32[32]{0:T(128)S(1)} %get-tuple-element.530, f32[32]{0:T(128)S(1)} %multiply_reduce_fusion.1), channel_id=1, replica_groups=mesh['gx'=32,'gy'=16] {'gx','gy'}, use_global_device_ids=true, to_apply=%region_1.2 | all-reduce | flops 64 | bytes 512 | tf_op jit(solution)/shard_map/psum | solution.py:128
  139.4 1.7 collective-permute-start.4
  141.1 1.3 collective-permute-start.5
  142.8 3.4 collective-permute-done.5
  146.2 5.3 collective-permute-start.6
  151.4 1.9 collective-permute-start.7
  153.3 1.6 fusion.103
  155.0 2.2 collective-permute-done.7
  157.4 1.2 fusion.36
  158.6 1.9 fusion.59
  160.7 263.5 %all-reduce.4.cloned.1.call-done = (f32[96,96]{1,0:T(8,128)}, f32[96,96]{1,0:T(8,128)}) async-done(((f32[96,96]{1,0:T(8,128)}, f32[96,96]{1,0:T(8,128)}), (f32[96,96]{1,0:T(8,128)}, f32[96,96]{1,0:T(8,128)})) %all-reduce.4.cloned.1.call-update) | async-done | bytes 73744 | tf_op jit(solution)/shard_map/psum | solution.py:110
  424.2 0.8 broadcast_multiply_fusion
  425.1 157.1 %while.60 = (s32[]{:T(128)}, f32[96,96]{1,0:T(8,128)S(1)}, f32[96,96]{0,1:T(8,128)S(1)}, s32[]{:T(128)}, s32[]{:T(128)}) while((s32[]{:T(128)}, f32[96,96]{1,0:T(8,128)S(1)}, f32[96,96]{0,1:T(8,128)S(1)}, s32[]{:T(128)}, s32[]{:T(128)}) %tuple.159), condition=%wide.region_7.8_spmd.clone.clone, body=%wide.region_5.7_spmd.clone.clone.sunk | while | flops 139010 | bytes 200992 | solution.py:71
  426.7 0.8 select_reduce_fusion.4
  428.4 0.8 select_reduce_fusion.4
  430.0 0.8 select_reduce_fusion.4
  431.6 0.8 select_reduce_fusion.4
  433.3 0.8 select_reduce_fusion.4
  434.9 0.8 select_reduce_fusion.4
  582.2 146.3 %while.58 = (s32[]{:T(128)}, f32[96,96]{1,0:T(8,128)S(1)}, f32[96,96]{1,0:T(8,128)S(1)}, f32[96,96]{1,0:T(8,128)S(1)}, s32[]{:T(128)}, /*index=5*/s32[]{:T(128)}) while((s32[]{:T(128)}, f32[96,96]{1,0:T(8,128)S(1)}, f32[96,96]{1,0:T(8,128)S(1)}, f32[96,96]{1,0:T(8,128)S(1)}, s32[]{:T(128)}, /*index=5*/s32[]{:T(128)}) %tuple.162), condition=%wide.region_10.11_spmd.clone, body=%wide.region_8.10_spmd.clone.sunk | while | flops 138818 | bytes 127896 | solution.py:86
  729.8 0.8 convolution_subtract_fusion
  730.8 49.6 %while.61 = (s32[]{:T(128)}, f32[32,32]{1,0:T(8,128)S(1)}, f32[32,32]{0,1:T(8,128)S(1)}, s32[]{:T(128)}, s32[]{:T(128)}) while((s32[]{:T(128)}, f32[32,32]{1,0:T(8,128)S(1)}, f32[32,32]{0,1:T(8,128)S(1)}, s32[]{:T(128)}, s32[]{:T(128)}) %tuple.165), condition=%wide.region_16.17_spmd.clone.clone, body=%wide.region_14.16_spmd.clone.clone.sunk | while | flops 15618 | bytes 36000 | solution.py:71
  780.4 47.1 %while.59 = (s32[]{:T(128)}, f32[32,32]{1,0:T(8,128)S(1)}, f32[32,32]{1,0:T(8,128)S(1)}, f32[32,32]{1,0:T(8,128)S(1)}, s32[]{:T(128)}, /*index=5*/s32[]{:T(128)}) while((s32[]{:T(128)}, f32[32,32]{1,0:T(8,128)S(1)}, f32[32,32]{1,0:T(8,128)S(1)}, f32[32,32]{1,0:T(8,128)S(1)}, s32[]{:T(128)}, /*index=5*/s32[]{:T(128)}) %tuple.168), condition=%wide.region_19.20_spmd.clone, body=%wide.region_17.19_spmd.clone.sunk | while | flops 15554 | bytes 28696 | solution.py:86
  827.7 0.8 fusion.32
  (1213 shorter events, 307.1 us)
Async XLA Ops:
  7.2 1.2 copy-start.1
  7.2 417.0 %all-reduce.4.cloned.1.call-start = ((), (), s32[]{:S(2)}) async-start(), calls=%async_computation | async-start | bytes 196608 | tf_op jit(solution)/shard_map/psum | solution.py:110
  8.4 0.7 copy-start.4
  9.4 5.4 copy-start
  9.6 5.6 collective-permute-start
  13.5 5.0 collective-permute-start.1
  18.7 8.6 %collective-permute-start.2 = (f32[65,10,1,16]{0,3,2,1:T(8,128)S(1)}, f32[65,10,1,16]{0,3,2,1:T(8,128)S(1)}, u32[]{:S(2)}, u32[]{:S(2)}) collective-permute-start(f32[65,10,1,16]{0,3,2,1:T(8,128)S(1)} %get-tuple-element.505), channel_id=1, source_target_pairs={{0,1},{1,2},{2,3},{3,4},{4,5},{5,6},{6,7},{7,8},{8,9},{9,10},{10,1... | collective-permute-start | bytes 124808 | tf_op jit(solution)/shard_map/ppermute | solution.py:17
  23.9 5.8 collective-permute-start.3
  139.4 3.4 collective-permute-start.4
  141.1 5.0 collective-permute-start.5
  146.2 8.8 %collective-permute-start.6 = (f32[32,10,1,16]{0,3,2,1:T(8,128)S(1)}, f32[32,10,1,16]{0,3,2,1:T(8,128)S(1)}, u32[]{:S(2)}, u32[]{:S(2)}) collective-permute-start(f32[32,10,1,16]{0,3,2,1:T(8,128)S(1)} %get-tuple-element.525), channel_id=1, source_target_pairs={{0,1},{1,2},{2,3},{3,4},{4,5},{5,6},{6,7},{7,8},{8,9},{9,10},{10,1... | collective-permute-start | bytes 61448 | tf_op jit(solution)/shard_map/ppermute | solution.py:17
  151.4 5.8 collective-permute-start.7
  582.2 146.3 %copy-start.2 = (f32[96,96]{1,0:T(8,128)S(1)}, f32[96,96]{1,0:T(8,128)}, u32[]{:S(2)}) copy-start(f32[96,96]{1,0:T(8,128)} %get-tuple-element.498) | copy-start | bytes 110596
  729.1 0.7 copy-start.3
Sparse Core Ops, SparseCore 0:
  160.7 263.3 all-reduce.3
where the time goes:
time: 843 us; the launch traced here: 838 us
  waiting for transfers between devices  275 us (33%)
  matrix products  209 us (25%)
  other arithmetic  107 us (13%)
  blocking collectives  107 us (13%)
  loops' own time  97 us (12%)
  starting transfers between devices  24 us (3%)
  between operations  14.5 us (2%)
    psum x1, waiting for transfers between devices, sum_pair(): return lax.psum((gram_part, proj_part), ('gx', 'gy'))  264 us
    psum x1, blocking collectives, body(): lax.psum((jnp.sum(basis_flat * image_x, 1), jnp.sum(basis_flat * basis_fl...  107 us
    dot_general x128, matrix products, row(): fresh_row = (e_row - jnp.dot(l_row, result, precision=HIGH)) / pivot  101 us
    dot_general x128, matrix products, column(): vec = col_a - jnp.dot(lower, row_j, precision=HIGH)  101 us
    another operation x2, loops' own time, chol_lower(): return lax.fori_loop(0, size, column, jnp.zeros_like(matrix))  93.7 us
    reduce_sum x128, other arithmetic, row(): pivot = jnp.sum(jnp.where(index == i, l_row, 0.0))  77.6 us
  transfers between devices with their start and end apart: 9, of which 5 were waited for; matrix products, arithmetic and copies ran while one was open for 0% of the time, Pallas kernels for 0%

commit v1 on v0

v1 whole, which is shorter than its diff:
```python
import jax
import jax.numpy as jnp
import numpy as np
from jax import lax
from jax.experimental import pallas as pl
from jax.experimental.pallas import tpu as pltpu
from jax.sharding import PartitionSpec as P

CZ = 16
MODES = 32
ROWS = 8
LANES = 128
HIGH = lax.Precision.HIGHEST
VMEM = pl.BlockSpec(memory_space=pltpu.VMEM)


def dot_nt(left, right):
    return lax.dot_general(
        left, right, (((1,), (1,)), ((), ())), precision=HIGH, preferred_element_type=jnp.float32
    )


def dot_nn(left, right):
    return lax.dot_general(
        left, right, (((1,), (0,)), ((), ())), precision=HIGH, preferred_element_type=jnp.float32
    )


def roll(array, shift):
    shift = shift % LANES
    return pltpu.roll(array, shift, array.ndim - 1) if shift else array


def lanes(shape):
    return lax.broadcasted_iota(jnp.int32, shape, len(shape) - 1)


def pack_rows(basis_hbm, search_hbm, cond_hbm, up, down, basis, search, cond, arrived):
    copies = [
        pltpu.make_async_copy(source, target, arrived.at[k])
        for k, (source, target) in enumerate(
            ((basis_hbm, basis), (search_hbm, search), (cond_hbm, cond))
        )
    ]
    for copy in copies:
        copy.start()
    for copy in copies:
        copy.wait()
    for message, first, second, edge in ((up, 6, 7, 7), (down, 0, 1, 0)):
        message[0:32, :] = basis[:, first, :]
        message[32:64, :] = basis[:, second, :]
        message[64:96, :] = search[:, edge, :]
        message[96:104, :] = cond[...]


def pack_sides(basis, search, cond, lo, hi, right, left):
    fields = [lo[32:64, :]] + [basis[:, s, :] for s in range(ROWS)] + [hi[0:32, :]]
    fields += [search[:, s, :] for s in range(ROWS)]
    conds = [lo[103:104, :]] + [cond[s : s + 1, :] for s in range(ROWS)] + [hi[96:97, :]]
    for message, base in ((right, 32), (left, 0)):
        for rows, start, step in ((fields, 0, 32), (conds, 160, 1)):
            for tile in range((len(rows) + 3) // 4):
                packed = None
                for k, row in enumerate(rows[4 * tile : 4 * tile + 4]):
                    if step == 1:
                        row = jnp.broadcast_to(row, (8, LANES))
                    moved = roll(row, base + 32 * k)
                    if packed is None:
                        packed = moved
                    else:
                        packed = jnp.where(lanes(moved.shape) >= 32 * k, moved, packed)
                message[start + step * tile : start + step * (tile + 1), :] = packed[:step]
        message[163:168, :] = jnp.zeros((5, LANES), jnp.float32)


def side_tile(low, high, index, start, step):
    tile, k = divmod(index, 4)
    place = start + step * tile
    below = low[place : place + step, :]
    above = high[place : place + step, :]
    if step == 1:
        below = jnp.broadcast_to(below, (8, LANES))
        above = jnp.broadcast_to(above, (8, LANES))
    lane = lanes(below.shape)
    below = roll(below, 96 - 32 * k)
    above = roll(above, -32 * k)
    return jnp.where(lane >= 96, below, jnp.where(lane < 32, above, 0.0))


def next_y(own, side):
    lane = lanes(own.shape)
    a, b = roll(own, -CZ), roll(side, -CZ)
    return jnp.where(lane < LANES - CZ, a, b), jnp.where(lane < LANES - CZ, b, a)


def prev_y(own, side):
    lane = lanes(own.shape)
    a, b = roll(own, CZ), roll(side, CZ)
    return jnp.where(lane >= CZ, a, b), jnp.where(lane >= CZ, b, a)


def next_z(array):
    return jnp.where(lanes(array.shape) % CZ == CZ - 1, roll(array, CZ - 1), roll(array, -1))


def prev_z(array):
    return jnp.where(lanes(array.shape) % CZ == 0, roll(array, 1 - CZ), roll(array, 1))


def images(basis, search, cond, lo, hi, low, high, fields, sums, conds, coef, image, stack):
    conds[...] = jnp.zeros_like(conds)
    conds[0, 0:2, :] = lo[102:104, :]
    conds[0, 2:10, :] = cond[...]
    conds[0, 10:12, :] = hi[96:98, :]
    for r in range(10):
        conds[1, r + 1 : r + 2, :] = side_tile(low, high, r, 160, 1)[:1]
    cond_a, cond_b = conds[0, 0:16, :], conds[1, 0:16, :]
    after = next_y(cond_a, cond_b)
    before = prev_y(cond_a, cond_b)
    for part, array in ((0, cond_a), (1, cond_b)):
        coef[part, 0] = 0.5 * (array + conds[part, 1:17, :])
        coef[part, 1] = 0.5 * (array + after[part])
        coef[part, 2] = 0.5 * (array + before[part])
        coef[part, 3] = 0.5 * (array + next_z(array))
        coef[part, 4] = 0.5 * (array + prev_z(array))

    def operator(part, r, own, beside, x_low, x_high):
        i = r + 2
        total = coef[part, 0, i - 1 : i, :] * (own - x_low)
        total += coef[part, 0, i : i + 1, :] * (own - x_high)
        total += coef[part, 1, i : i + 1, :] * (own - beside[0])
        total += coef[part, 2, i : i + 1, :] * (own - beside[1])
        total += coef[part, 3, i : i + 1, :] * (own - next_z(own))
        total += coef[part, 4, i : i + 1, :] * (own - prev_z(own))
        return total

    def beside(own, side):
        after, before = next_y(own, side), prev_y(own, side)
        return ((after[0], before[0]), (after[1], before[1]))

    def basis_row(r):
        if r < 0:
            return lo[32 * (r + 2) : 32 * (r + 3), :]
        if r >= ROWS:
            return hi[32 * (r - ROWS) : 32 * (r - ROWS + 1), :]
        return basis[:, r, :]

    def valid(part, r, array):
        return jnp.where(conds[part, r + 2 : r + 3, :] > 0.0, array, 0.0)

    sides = {r: side_tile(low, high, r + 1, 0, 32) for r in range(-1, 2)}
    for r in range(-1, ROWS + 1):
        if 1 <= r < ROWS:
            sides[r + 1] = side_tile(low, high, r + 2, 0, 32)
        own = basis_row(r)
        pairs = beside(own, sides[r])
        first = operator(0, r, own, pairs[0], basis_row(r - 1), basis_row(r + 1))
        image[0, r + 1] = first if 0 <= r < ROWS else valid(0, r, first)
        if 0 <= r < ROWS:
            second = operator(1, r, sides[r], pairs[1], sides[r - 1], sides[r + 1])
            image[1, r + 1] = valid(1, r, second)

    for s in range(ROWS):
        at = slice(LANES * s, LANES * (s + 1))
        field = search[:, s, :]
        pairs = beside(field, side_tile(low, high, 10 + s, 0, 32))
        x_low = lo[64:96, :] if s == 0 else search[:, s - 1, :]
        x_high = hi[64:96, :] if s == ROWS - 1 else search[:, s + 1, :]
        stack[128:160, at] = operator(0, s, field, pairs[0], x_low, x_high)
        own = image[0, s + 1]
        pairs = beside(own, image[1, s + 1])
        stack[96:128, at] = operator(0, s, own, pairs[0], image[0, s], image[0, s + 2])
        stack[0:32, at] = basis[:, s, :]
        stack[32:64, at] = own
        stack[64:96, at] = field
        fields[0:32, at] = basis[:, s, :]
        fields[32:64, at] = own
        fields[64:96, at] = field

    product = dot_nt(stack[0:96, :], stack[...])
    last = product[64:96, 128:160]
    sums[0:32, :] = jnp.concatenate([product[0:32, 0:96], last], 1)
    sums[32:64, :] = jnp.concatenate([product[64:96, 96:128], product[32:64, 32:128]], 1)
    corner = product[64:96, 64:96]
    sums[64:72, :] = jnp.concatenate([corner[8 * k : 8 * k + 8] for k in range(4)], 1)
    sums[72:128, :] = jnp.zeros((56, LANES), jnp.float32)


def eliminate(slabs):
    slabs = list(slabs)
    count = len(slabs)
    lane = lanes((8, LANES))
    row = lax.broadcasted_iota(jnp.int32, (8, LANES), 0)
    width = 4
    for start in range(0, 8 * count, width):
        g = start // 8
        cols = [
            {i: jnp.broadcast_to(slabs[i][:, start + k : start + k + 1], (8, LANES)) for i in range(g, count)}
            for k in range(width)
        ]
        for k in range(width):
            j = start + k
            at = j % 8
            pivot = cols[k][g][at : at + 1, :]
            inverse = 1.0 / pivot
            root = lax.rsqrt(pivot)
            here = lane[:1] == j
            pivot_row = jnp.where(here, 1.0, slabs[g][at : at + 1, :])
            scaled = pivot_row * inverse
            later = [cols[m][g][at : at + 1, :] * inverse for m in range(k + 1, width)]
            for i in range(g, count):
                factor = cols[k][i]
                kept = jnp.where(lane == j, 0.0, slabs[i])
                if i == g:
                    factor = jnp.where(row > at, factor, 0.0)
                    kept = jnp.where(row > at, kept, slabs[i])
                    fresh = kept - factor * scaled
                    slabs[i] = jnp.where(row == at, pivot_row * root, fresh)
                else:
                    slabs[i] = kept - factor * scaled
                for m in range(k + 1, width):
                    cols[m][i] = cols[m][i] - factor * later[m - k - 1]
    return slabs


def lower_part(slabs, size):
    whole = jnp.concatenate(slabs, 0)
    row = lax.broadcasted_iota(jnp.int32, whole.shape, 0)
    return jnp.where(lanes(whole.shape) <= row, whole, 0.0)[:, :size]


def update(scale, sums, start, fields, new_basis, new_search, values):
    first = sums[0:32, :] * scale
    second = sums[32:64, :] * scale
    third = sums[64:72, :] * scale
    xx, xy, xp, pr = (first[:, 32 * k : 32 * k + 32] for k in range(4))
    pz, yy, yp, yz = (second[:, 32 * k : 32 * k + 32] for k in range(4))
    pp = jnp.concatenate([third[:, 32 * k : 32 * k + 32] for k in range(4)], 0)
    px, py, zp = xp.T, yp.T, pz.T
    zero = jnp.zeros((32, 32), jnp.float32)
    gram = [
        jnp.concatenate([xx, xy, xp, zero], 1),
        jnp.concatenate([xy, yy, yp, zero], 1),
        jnp.concatenate([px, py, pp, zero], 1),
    ]
    projected = jnp.concatenate(
        [
            jnp.concatenate([xy, yy, yp], 1),
            jnp.concatenate([yy, yz, zp], 1),
            jnp.concatenate([py, pz, pr], 1),
        ],
        0,
    )
    lower_inv = lower_part(
        eliminate([block[8 * k : 8 * k + 8] for block in gram for k in range(4)]), 96
    )
    ritz = dot_nt(dot_nn(lower_inv, projected), lower_inv)
    ritz = 0.5 * (ritz + ritz.T)
    bound = jnp.max(jnp.sum(jnp.abs(ritz), 0, keepdims=True), 1, keepdims=True)
    seed = start[...].astype(jnp.float32)
    moved = bound * seed - dot_nn(seed, ritz)
    square = jnp.concatenate([dot_nt(moved, moved), jnp.zeros((32, 96), jnp.float32)], 1)
    small_inv = lower_part(eliminate([square[8 * k : 8 * k + 8] for k in range(4)]), 32)
    coeffs = dot_nn(small_inv, moved)
    weights = dot_nn(coeffs, lower_inv)
    terms = coeffs * dot_nn(coeffs, ritz)
    values[...] = dot_nt(jnp.ones((8, 96), jnp.float32), terms)[0:1, :]
    diagonal = lanes((32, 32)) == lax.broadcasted_iota(jnp.int32, (32, 32), 0)
    along = jnp.sum(jnp.where(diagonal, xy, 0.0), 0, keepdims=True)
    norms = jnp.sum(jnp.where(diagonal, xx, 0.0), 0, keepdims=True)
    quotient = along / norms
    middle = weights[:, 32:64]
    search_weights = jnp.concatenate([-(middle * quotient), middle, weights[:, 64:96]], 1)
    both = jnp.concatenate([weights, search_weights], 0)
    result = dot_nn(both, fields[...])
    for s in range(ROWS):
        new_basis[:, s, :] = result[0:32, LANES * s : LANES * (s + 1)]
        new_search[:, s, :] = result[32:64, LANES * s : LANES * (s + 1)]


def call(kernel, outs, *args, scratch=(), place=VMEM, room=32):
    shapes = [jax.ShapeDtypeStruct(shape, jnp.float32) for shape in outs]
    return pl.pallas_call(
        kernel,
        out_shape=shapes,
        in_specs=[place] * len(args),
        out_specs=[VMEM] * len(shapes),
        scratch_shapes=[
            pltpu.VMEM(shape, jnp.float32) if isinstance(shape, tuple) else shape for shape in scratch
        ],
        compiler_params=pltpu.CompilerParams(vmem_limit_bytes=room * 1024 * 1024),
    )(*args)


def shifted(array, axis, step):
    count = lax.axis_size(axis)
    return lax.ppermute(array, axis, [(i, i + step) for i in range(count) if 0 <= i + step < count])


def summed(array, count):
    return jnp.sum(array.reshape(count, array.shape[0] // count, LANES), 0)


def groups(sizes, free):
    index = np.arange(int(np.prod(sizes))).reshape(sizes)
    kept = [axis for axis in range(len(sizes)) if axis not in free]
    count = int(np.prod([sizes[axis] for axis in free]))
    return index.transpose(kept + list(free)).reshape(-1, count).tolist()


def total(array):
    along, across = lax.axis_size("gx"), lax.axis_size("gy")
    sizes = (along // 4, 4, across // 2, 2)

    def exchanged(parts, free):
        return lax.all_to_all(
            parts, ("gx", "gy"), 0, 0, axis_index_groups=groups(sizes, free), tiled=True
        )

    share = summed(exchanged(array, (1, 3)), 8)
    for axis in (2, 0):
        share = summed(exchanged(jnp.tile(share, (sizes[axis], 1)), (axis,)), sizes[axis])
    return exchanged(jnp.tile(share, (8, 1)), (1, 3))


def body(basis, search, conductivity, rotation):
    modes, cells_x, flat = basis.shape
    count = cells_x * flat * lax.axis_size("gx") * lax.axis_size("gy")
    blocks = [basis.shape, search.shape, conductivity.shape]
    up, down = call(
        pack_rows,
        [(104, LANES)] * 2,
        basis,
        search,
        conductivity,
        scratch=blocks + [pltpu.SemaphoreType.DMA((3,))],
        place=pl.BlockSpec(memory_space=pl.ANY),
        room=63,
    )
    lo, hi = shifted(up, "gx", 1), shifted(down, "gx", -1)
    right, left = call(pack_sides, [(168, LANES)] * 2, basis, search, conductivity, lo, hi)
    low, high = shifted(right, "gy", 1), shifted(left, "gy", -1)
    fields, sums = call(
        images,
        [(96, ROWS * LANES), (LANES, LANES)],
        basis,
        search,
        conductivity,
        lo,
        hi,
        low,
        high,
        scratch=[(2, 24, LANES), (2, 5, 16, LANES), (2, 10, MODES, LANES), (160, ROWS * LANES)],
    )
    sums = total(sums)

    def finish(*refs):
        update(1.0 / count, *refs)

    new_basis, new_search, values = call(
        finish,
        [(modes, cells_x, flat), (modes, cells_x, flat), (1, modes)],
        sums,
        rotation.T,
        fields,
    )
    return new_basis, new_search, values.reshape(modes)


def solution(mesh):
    in_specs = (P(None, "gx", "gy"), P(None, "gx", "gy"), P("gx", "gy"), P())
    out_specs = (P(None, "gx", "gy"), P(None, "gx", "gy"), P())
    return jax.shard_map(body, mesh=mesh, in_specs=in_specs, out_specs=out_specs, check_vma=False)
```

time: 843 us -> 84.9 us (0.10)
  waiting for transfers between devices: 275 us -> 6.19 us
  matrix products: 209 us -> 0 us
  other arithmetic: 107 us -> 0.03 us
  loops' own time: 97 us -> 0 us
  blocking collectives: 107 us -> 53 us
  between operations: 14.5 us -> 0.76 us
  Pallas kernels: 0 us -> 10.7 us
  starting transfers between devices: 24 us -> 13.8 us
    psum x1 -> x0, waiting for transfers between devices: 264 us -> none  [sum_pair(): return lax.psum((gram_part, proj_part), ('gx', 'gy'))]
    dot_general x267 -> x0, matrix products: 209 us -> none  [the longest x128 101 us: row(): fresh_row = (e_row - jnp.dot(l_row, result, precision=HIGH)) / pivot]
    psum x1 -> x0, blocking collectives: 107 us -> none  [body(): lax.psum((jnp.sum(basis_flat * image_x, 1), jnp.sum(basis_flat * basis_fl...]
    another operation x4 -> x0, loops' own time: 97 us -> none  [the longest x2 93.7 us: chol_lower(): return lax.fori_loop(0, size, column, jnp.zeros_like(matrix))]
    reduce_sum x130 -> x3, other arithmetic: 78.1 us -> 0.03 us  [summed(): return jnp.sum(array.reshape(count, array.shape[0] // count, LANES), 0)]
    all_to_all x0 -> x4, blocking collectives: none -> 53 us  [exchanged(): lax.all_to_all(parts, ('gx', 'gy'), 0, 0, axis_index_groups=groups(sizes,...]
    select_n x384 -> x0, other arithmetic: 21 us -> none  [the longest x128 10.4 us: row(): return jnp.where(index[:, None] == i, fresh_row[None, :], result)]
    pallas_call x0 -> x4, Pallas kernels: none -> 10.7 us  [call(): pl.pallas_call(kernel, out_shape=shapes, in_specs=[place] * len(args), ou...]
  transfers between devices with their start and end apart: 9 -> 4, of which waited for: 5 -> 3; matrix products, arithmetic and copies ran while one was open for 0% -> 0% of each run, Pallas kernels for 0% -> 0%
where the time goes in v1:
time: 84.9 us; the launch traced here: 84.5 us
  blocking collectives  53 us (62%)
  starting transfers between devices  13.8 us (16%)
  Pallas kernels  10.7 us (13%)
  waiting for transfers between devices  6.19 us (7%)
    all_to_all x4, blocking collectives, exchanged(): lax.all_to_all(parts, ('gx', 'gy'), 0, 0, axis_index_groups=groups(sizes,...  53 us
    ppermute x4, starting transfers between devices, shifted(): lax.ppermute(array, axis, [(i, i + step) for i in range(count) if 0 <= i...  13.8 us
    pallas_call x4, Pallas kernels, call(): pl.pallas_call(kernel, out_shape=shapes, in_specs=[place] * len(args), ou...  10.7 us
    ppermute x4, waiting for transfers between devices, shifted(): lax.ppermute(array, axis, [(i, i + step) for i in range(count) if 0 <= i...  6.19 us
  transfers between devices with their start and end apart: 4, of which 3 were waited for; matrix products, arithmetic and copies ran while one was open for 0% of the time, Pallas kernels for 0%

profile of v1, /device:TPU:1, one launch (start us, length us, event | category | flops | bytes accessed | tf_op | source)
XLA Modules:
  0.0 84.5 jit_solution(17824185393822138189)
XLA Ops:
  0.6 0.0 copy-start.1
  0.6 0.0 copy-start
  0.7 0.0 copy-start.2
  0.7 1.7 %shard_map.67 = (f32[104,128]{1,0:T(8,128)}, f32[104,128]{1,0:T(8,128)}) custom-call(f32[32,8,128]{2,1,0:T(8,128)} %basis.3, f32[32,8,128]{2,1,0:T(8,128)} %search.3, f32[8,128]{1,0:T(8,128)} %cond.3), custom_call_target="tpu_custom_call" | custom-call | tf_op jit(solution)/shard_map/pallas_call | solution.py:283
  2.4 3.9 %collective-permute-start = (f32[104,128]{1,0:T(8,128)}, f32[104,128]{1,0:T(8,128)S(1)}, u32[]{:S(2)}, u32[]{:S(2)}) collective-permute-start(f32[104,128]{1,0:T(8,128)} %get-tuple-element.12), channel_id=1, source_target_pairs={{0,16},{16,32},{32,48},{48,64},{64,80},{80,96},{96,112},{112,128},... | collective-permute-start | bytes 159752 | tf_op jit(solution)/shard_map/ppermute | solution.py:297
  6.4 1.3 %collective-permute-start.1 = (f32[104,128]{1,0:T(8,128)}, f32[104,128]{1,0:T(8,128)S(1)}, u32[]{:S(2)}, u32[]{:S(2)}) collective-permute-start(f32[104,128]{1,0:T(8,128)} %get-tuple-element.13), channel_id=1, source_target_pairs={{16,0},{32,16},{48,32},{64,48},{80,64},{96,80},{112,96},{128,112},... | collective-permute-start | bytes 159752 | tf_op jit(solution)/shard_map/ppermute | solution.py:297
  7.7 0.2 collective-permute-done.lo
  7.9 3.6 %collective-permute-done.1.hi = f32[104,128]{1,0:T(8,128)S(1)} collective-permute-done((f32[104,128]{1,0:T(8,128)}, f32[104,128]{1,0:T(8,128)S(1)}, u32[]{:S(2)}, u32[]{:S(2)}) %collective-permute-start.1) | collective-permute-done | bytes 53280 | tf_op jit(solution)/shard_map/ppermute | solution.py:297
  11.4 0.0 copy-done.1
  11.4 0.0 copy-done
  11.4 0.0 copy-done.2
  11.4 0.2 shard_map.68
  11.7 5.2 %collective-permute-start.2 = (f32[168,128]{1,0:T(8,128)S(1)}, f32[168,128]{1,0:T(8,128)S(1)}, u32[]{:S(2)}, u32[]{:S(2)}) collective-permute-start(f32[168,128]{1,0:T(8,128)S(1)} %get-tuple-element.14), channel_id=1, source_target_pairs={{0,1},{1,2},{2,3},{3,4},{4,5},{5,6},{6,7},{7,8},{8,9},{9,10},{10,1... | collective-permute-start | bytes 258056 | tf_op jit(solution)/shard_map/ppermute | solution.py:297
  16.9 3.4 %collective-permute-start.3 = (f32[168,128]{1,0:T(8,128)S(1)}, f32[168,128]{1,0:T(8,128)S(1)}, u32[]{:S(2)}, u32[]{:S(2)}) collective-permute-start(f32[168,128]{1,0:T(8,128)S(1)} %get-tuple-element.15), channel_id=1, source_target_pairs={{1,0},{2,1},{3,2},{4,3},{5,4},{6,5},{7,6},{8,7},{9,8},{10,9},{11,1... | collective-permute-start | bytes 258056 | tf_op jit(solution)/shard_map/ppermute | solution.py:297
  20.3 0.0 collective-permute-done.2.low
  20.3 2.4 %collective-permute-done.3.high = f32[168,128]{1,0:T(8,128)S(1)} collective-permute-done((f32[168,128]{1,0:T(8,128)S(1)}, f32[168,128]{1,0:T(8,128)S(1)}, u32[]{:S(2)}, u32[]{:S(2)}) %collective-permute-start.3) | collective-permute-done | bytes 86048 | tf_op jit(solution)/shard_map/ppermute | solution.py:297
  22.7 2.0 %shard_map.69 = (f32[96,1024]{1,0:T(8,128)S(1)}, f32[128,128]{1,0:T(8,128)S(1)}) custom-call(f32[32,8,128]{2,1,0:T(8,128)S(1)} %copy-done, f32[32,8,128]{2,1,0:T(8,128)S(1)} %copy-done.1, f32[8,128]{1,0:T(8,128)S(1)} %copy-done.2, f32[104,128]{1,0:T(8,128)S(1)} %collective-permute-done.lo, f32[104,128]{1,0:T(8,128)S(1)} %collective-permute-done.1.hi, ...), custom_call_target="tpu_custom_call" | custom-call | tf_op jit(solution)/shard_map/pallas_call | solution.py:283
  24.7 11.7 %all_to_all.29 = f32[8,16,128]{2,1,0:T(8,128)S(1)} all-to-all(f32[8,16,128]{2,1,0:T(8,128)S(1)} %bitcast.5), channel_id=1, replica_groups={{0,1,16,17,32,33,48,49},{2,3,18,19,34,35,50,51},{4,5,20,21,36,37,52,53}..., dimensions={0} | all-to-all | bytes 131072 | tf_op jit(solution)/shard_map/all_to_all | solution.py:316
  36.4 14.1 %all_to_all.30 = f32[8,16,128]{2,1,0:T(8,128)S(1)} all-to-all(f32[8,16,128]{2,1,0:T(8,128)S(1)} %tile.6), channel_id=1, replica_groups={{0,2,4,6,8,10,12,14},{1,3,5,7,9,11,13,15},{16,18,20,22,24,26,28,30},{17..., dimensions={0} | all-to-all | bytes 131072 | tf_op jit(solution)/shard_map/all_to_all | solution.py:316
  50.5 16.4 %all_to_all.31 = f32[8,16,128]{2,1,0:T(8,128)S(1)} all-to-all(f32[8,16,128]{2,1,0:T(8,128)S(1)} %tile.7), channel_id=1, replica_groups={{0,64,128,192,256,320,384,448},{1,65,129,193,257,321,385,449},{2,66,130..., dimensions={0} | all-to-all | bytes 131072 | tf_op jit(solution)/shard_map/all_to_all | solution.py:316
  66.9 0.0 copy-start.3
  66.9 10.9 %all_to_all.32 = f32[8,16,128]{2,1,0:T(8,128)S(1)} all-to-all(f32[8,16,128]{2,1,0:T(8,128)S(1)} %tile.8), channel_id=1, replica_groups={{0,1,16,17,32,33,48,49},{2,3,18,19,34,35,50,51},{4,5,20,21,36,37,52,53}..., dimensions={0} | all-to-all | bytes 131072 | tf_op jit(solution)/shard_map/all_to_all | solution.py:316
  77.8 0.0 copy-done.3
  77.8 6.7 %shard_map.70 = (f32[32,8,128]{2,1,0:T(8,128)}, f32[32,8,128]{2,1,0:T(8,128)}, f32[1,32]{1,0:T(1,128)}) custom-call(f32[128,128]{1,0:T(8,128)S(1)} %bitcast.4, s32[32,96]{1,0:T(8,128)S(1)} %bitcast.6, f32[96,1024]{1,0:T(8,128)S(1)} %get-tuple-element.17.refs_2_), custom_call_target="tpu_custom_call" | custom-call | tf_op jit(solution)/shard_map/pallas_call | solution.py:283
  (6 shorter events, 0.1 us)
Async XLA Ops:
  0.6 10.8 %copy-start.1 = (f32[32,8,128]{2,1,0:T(8,128)S(1)}, f32[32,8,128]{2,1,0:T(8,128)}, u32[]{:S(2)}) copy-start(f32[32,8,128]{2,1,0:T(8,128)} %search.3) | copy-start | bytes 393220
  0.6 10.8 %copy-start = (f32[32,8,128]{2,1,0:T(8,128)S(1)}, f32[32,8,128]{2,1,0:T(8,128)}, u32[]{:S(2)}) copy-start(f32[32,8,128]{2,1,0:T(8,128)} %basis.3) | copy-start | bytes 393220
  0.7 10.8 %copy-start.2 = (f32[8,128]{1,0:T(8,128)S(1)}, f32[8,128]{1,0:T(8,128)}, u32[]{:S(2)}) copy-start(f32[8,128]{1,0:T(8,128)} %cond.3) | copy-start | bytes 12292
  2.4 5.5 %collective-permute-start = (f32[104,128]{1,0:T(8,128)}, f32[104,128]{1,0:T(8,128)S(1)}, u32[]{:S(2)}, u32[]{:S(2)}) collective-permute-start(f32[104,128]{1,0:T(8,128)} %get-tuple-element.12), channel_id=1, source_target_pairs={{0,16},{16,32},{32,48},{48,64},{64,80},{80,96},{96,112},{112,128},... | collective-permute-start | bytes 159752 | tf_op jit(solution)/shard_map/ppermute | solution.py:297
  6.4 5.1 %collective-permute-start.1 = (f32[104,128]{1,0:T(8,128)}, f32[104,128]{1,0:T(8,128)S(1)}, u32[]{:S(2)}, u32[]{:S(2)}) collective-permute-start(f32[104,128]{1,0:T(8,128)} %get-tuple-element.13), channel_id=1, source_target_pairs={{16,0},{32,16},{48,32},{64,48},{80,64},{96,80},{112,96},{128,112},... | collective-permute-start | bytes 159752 | tf_op jit(solution)/shard_map/ppermute | solution.py:297
  11.7 8.6 %collective-permute-start.2 = (f32[168,128]{1,0:T(8,128)S(1)}, f32[168,128]{1,0:T(8,128)S(1)}, u32[]{:S(2)}, u32[]{:S(2)}) collective-permute-start(f32[168,128]{1,0:T(8,128)S(1)} %get-tuple-element.14), channel_id=1, source_target_pairs={{0,1},{1,2},{2,3},{3,4},{4,5},{5,6},{6,7},{7,8},{8,9},{9,10},{10,1... | collective-permute-start | bytes 258056 | tf_op jit(solution)/shard_map/ppermute | solution.py:297
  16.9 5.8 %collective-permute-start.3 = (f32[168,128]{1,0:T(8,128)S(1)}, f32[168,128]{1,0:T(8,128)S(1)}, u32[]{:S(2)}, u32[]{:S(2)}) collective-permute-start(f32[168,128]{1,0:T(8,128)S(1)} %get-tuple-element.15), channel_id=1, source_target_pairs={{1,0},{2,1},{3,2},{4,3},{5,4},{6,5},{7,6},{8,7},{9,8},{10,9},{11,1... | collective-permute-start | bytes 258056 | tf_op jit(solution)/shard_map/ppermute | solution.py:297
  66.9 10.9 %copy-start.3 = (s32[96,32]{0,1:T(8,128)S(1)}, s32[96,32]{0,1:T(8,128)}, u32[]{:S(2)}) copy-start(s32[96,32]{0,1:T(8,128)} %param.7) | copy-start | bytes 36868

commit v2 on v1

--- a/solution.py
+++ b/solution.py
@@ -1,6 +1,5 @@
 import jax
 import jax.numpy as jnp
-import numpy as np
 from jax import lax
 from jax.experimental import pallas as pl
 from jax.experimental.pallas import tpu as pltpu
@@ -35,7 +34,17 @@
     return lax.broadcasted_iota(jnp.int32, shape, len(shape) - 1)
 
 
-def pack_rows(basis_hbm, search_hbm, cond_hbm, up, down, basis, search, cond, arrived):
+def is_odd(axis):
+    return lax.axis_index(axis) % 2 == 1
+
+
+def sort_sides(axis, one, two, low, high):
+    odd = is_odd(axis)
+    low[...] = jnp.where(odd, one[...], two[...])
+    high[...] = jnp.where(odd, two[...], one[...])
+
+
+def pack_rows(basis_hbm, search_hbm, cond_hbm, one, two, basis, search, cond, arrived):
     copies = [
         pltpu.make_async_copy(source, target, arrived.at[k])
         for k, (source, target) in enumerate(
@@ -46,14 +55,18 @@
         copy.start()
     for copy in copies:
         copy.wait()
-    for message, first, second, edge in ((up, 6, 7, 7), (down, 0, 1, 0)):
-        message[0:32, :] = basis[:, first, :]
-        message[32:64, :] = basis[:, second, :]
-        message[64:96, :] = search[:, edge, :]
-        message[96:104, :] = cond[...]
-
-
-def pack_sides(basis, search, cond, lo, hi, right, left):
+    up = [basis[:, 6, :], basis[:, 7, :], search[:, 7, :]]
+    down = [basis[:, 0, :], basis[:, 1, :], search[:, 0, :]]
+    odd = is_odd("gx")
+    for k in range(3):
+        one[32 * k : 32 * k + 32, :] = jnp.where(odd, down[k], up[k])
+        two[32 * k : 32 * k + 32, :] = jnp.where(odd, up[k], down[k])
+    one[96:104, :] = cond[...]
+    two[96:104, :] = cond[...]
+
+
+def pack_sides(basis, search, cond, row_one, row_two, side_one, side_two, lo, hi, right, left):
+    sort_sides("gx", row_one, row_two, lo, hi)
     fields = [lo[32:64, :]] + [basis[:, s, :] for s in range(ROWS)] + [hi[0:32, :]]
     fields += [search[:, s, :] for s in range(ROWS)]
     conds = [lo[103:104, :]] + [cond[s : s + 1, :] for s in range(ROWS)] + [hi[96:97, :]]
@@ -71,6 +84,7 @@
                         packed = jnp.where(lanes(moved.shape) >= 32 * k, moved, packed)
                 message[start + step * tile : start + step * (tile + 1), :] = packed[:step]
         message[163:168, :] = jnp.zeros((5, LANES), jnp.float32)
+    sort_sides("gy", left, right, side_one, side_two)
 
 
 def side_tile(low, high, index, start, step):
@@ -107,7 +121,10 @@
     return jnp.where(lanes(array.shape) % CZ == 0, roll(array, 1 - CZ), roll(array, 1))
 
 
-def images(basis, search, cond, lo, hi, low, high, fields, sums, conds, coef, image, stack):
+def images(
+    basis, search, cond, lo, hi, side_one, side_two, fields, sums, conds, coef, image, stack, low, high
+):
+    sort_sides("gy", side_one, side_two, low, high)
     conds[...] = jnp.zeros_like(conds)
     conds[0, 0:2, :] = lo[102:104, :]
     conds[0, 2:10, :] = cond[...]
@@ -292,42 +309,31 @@
     )(*args)
 
 
-def shifted(array, axis, step):
-    count = lax.axis_size(axis)
-    return lax.ppermute(array, axis, [(i, i + step) for i in range(count) if 0 <= i + step < count])
+def paired(array, axis, first):
+    pairs = [(i, i + 1) for i in range(first, lax.axis_size(axis) - 1, 2)]
+    return lax.ppermute(array, axis, pairs + [(j, i) for i, j in pairs])
+
+
+def exchanged(array, axis):
+    return lax.all_to_all(array, axis, 0, 0, tiled=True)
 
 
 def summed(array, count):
     return jnp.sum(array.reshape(count, array.shape[0] // count, LANES), 0)
 
 
-def groups(sizes, free):
-    index = np.arange(int(np.prod(sizes))).reshape(sizes)
-    kept = [axis for axis in range(len(sizes)) if axis not in free]
-    count = int(np.prod([sizes[axis] for axis in free]))
-    return index.transpose(kept + list(free)).reshape(-1, count).tolist()
-
-
 def total(array):
-    along, across = lax.axis_size("gx"), lax.axis_size("gy")
-    sizes = (along // 4, 4, across // 2, 2)
-
-    def exchanged(parts, free):
-        return lax.all_to_all(
-            parts, ("gx", "gy"), 0, 0, axis_index_groups=groups(sizes, free), tiled=True
-        )
-
-    share = summed(exchanged(array, (1, 3)), 8)
-    for axis in (2, 0):
-        share = summed(exchanged(jnp.tile(share, (sizes[axis], 1)), (axis,)), sizes[axis])
-    return exchanged(jnp.tile(share, (8, 1)), (1, 3))
+    across, along = lax.axis_size("gy"), lax.axis_size("gx")
+    share = summed(exchanged(array, "gy"), across)
+    share = summed(exchanged(jnp.tile(share, (along, 1)), "gx"), along)
+    return exchanged(jnp.tile(share, (across, 1)), "gy")
 
 
 def body(basis, search, conductivity, rotation):
     modes, cells_x, flat = basis.shape
     count = cells_x * flat * lax.axis_size("gx") * lax.axis_size("gy")
     blocks = [basis.shape, search.shape, conductivity.shape]
-    up, down = call(
+    rows = call(
         pack_rows,
         [(104, LANES)] * 2,
         basis,
@@ -337,9 +343,17 @@
         place=pl.BlockSpec(memory_space=pl.ANY),
         room=63,
     )
-    lo, hi = shifted(up, "gx", 1), shifted(down, "gx", -1)
-    right, left = call(pack_sides, [(168, LANES)] * 2, basis, search, conductivity, lo, hi)
-    low, high = shifted(right, "gy", 1), shifted(left, "gy", -1)
+    rows = [paired(rows[k], "gx", k) for k in range(2)]
+    side_one, side_two, lo, hi = call(
+        pack_sides,
+        [(168, LANES)] * 2 + [(104, LANES)] * 2,
+        basis,
+        search,
+        conductivity,
+        *rows,
+        scratch=[(168, LANES)] * 2,
+    )
+    side_one, side_two = paired(side_one, "gy", 0), paired(side_two, "gy", 1)
     fields, sums = call(
         images,
         [(96, ROWS * LANES), (LANES, LANES)],
@@ -348,9 +362,10 @@
         conductivity,
         lo,
         hi,
-        low,
-        high,
-        scratch=[(2, 24, LANES), (2, 5, 16, LANES), (2, 10, MODES, LANES), (160, ROWS * LANES)],
+        side_one,
+        side_two,
+        scratch=[(2, 24, LANES), (2, 5, 16, LANES), (2, 10, MODES, LANES), (160, ROWS * LANES)]
+        + [(168, LANES)] * 2,
     )
     sums = total(sums)
 

time: 84.9 us -> 82.1 us (0.967)
  blocking collectives: 53 us -> 49.4 us
  starting transfers between devices: 13.8 us -> 15.9 us
  waiting for transfers between devices: 6.19 us -> 4.92 us
    all_to_all x4 -> x3, blocking collectives: 53 us -> 49.4 us  [exchanged(): return lax.all_to_all(array, axis, 0, 0, tiled=True)]
    ppermute x4, starting transfers between devices: 13.8 us -> 15.9 us  [paired(): return lax.ppermute(array, axis, pairs + [(j, i) for i, j in pairs])]
    ppermute x4, waiting for transfers between devices: 6.19 us -> 4.92 us  [paired(): return lax.ppermute(array, axis, pairs + [(j, i) for i, j in pairs])]
  transfers between devices with their start and end apart: 4 -> 4, of which waited for: 3 -> 2; matrix products, arithmetic and copies ran while one was open for 0% -> 0% of each run, Pallas kernels for 0% -> 0%
where the time goes in v2:
time: 82.1 us; the launch traced here: 81.7 us
  blocking collectives  49.4 us (60%)
  starting transfers between devices  15.9 us (19%)
  Pallas kernels  10.7 us (13%)
  waiting for transfers between devices  4.92 us (6%)
    all_to_all x3, blocking collectives, exchanged(): return lax.all_to_all(array, axis, 0, 0, tiled=True)  49.4 us
    ppermute x4, starting transfers between devices, paired(): return lax.ppermute(array, axis, pairs + [(j, i) for i, j in pairs])  15.9 us
    pallas_call x4, Pallas kernels, call(): pl.pallas_call(kernel, out_shape=shapes, in_specs=[place] * len(args), ou...  10.7 us
    ppermute x4, waiting for transfers between devices, paired(): return lax.ppermute(array, axis, pairs + [(j, i) for i, j in pairs])  4.92 us
  transfers between devices with their start and end apart: 4, of which 2 were waited for; matrix products, arithmetic and copies ran while one was open for 0% of the time, Pallas kernels for 0%

profile of v2, /device:TPU:1, one launch (start us, length us, event | category | flops | bytes accessed | tf_op | source)
XLA Modules:
  0.0 81.7 jit_solution(9134084310959318950)
XLA Ops:
  0.6 0.0 copy-start.1
  0.6 0.0 copy-start
  0.7 0.0 copy-start.2
  0.7 1.8 %shard_map.67 = (f32[104,128]{1,0:T(8,128)}, f32[104,128]{1,0:T(8,128)}) custom-call(f32[32,8,128]{2,1,0:T(8,128)} %basis.3, f32[32,8,128]{2,1,0:T(8,128)} %search.3, f32[8,128]{1,0:T(8,128)} %cond.3), custom_call_target="tpu_custom_call" | custom-call | tf_op jit(solution)/shard_map/pallas_call | solution.py:300
  2.4 3.9 %collective-permute-start = (f32[104,128]{1,0:T(8,128)}, f32[104,128]{1,0:T(8,128)S(1)}, u32[]{:S(2)}, u32[]{:S(2)}) collective-permute-start(f32[104,128]{1,0:T(8,128)} %get-tuple-element.14), channel_id=1, source_target_pairs={{0,16},{32,48},{64,80},{96,112},{128,144},{160,176},{192,208},{224... | collective-permute-start | bytes 159752 | tf_op jit(solution)/shard_map/ppermute | solution.py:314
  6.4 0.7 collective-permute-start.1
  7.0 1.0 %collective-permute-done.row_one = f32[104,128]{1,0:T(8,128)S(1)} collective-permute-done((f32[104,128]{1,0:T(8,128)}, f32[104,128]{1,0:T(8,128)S(1)}, u32[]{:S(2)}, u32[]{:S(2)}) %collective-permute-start) | collective-permute-done | bytes 53280 | tf_op jit(solution)/shard_map/ppermute | solution.py:314
  8.1 0.0 collective-permute-done.1.row_two
  8.1 0.0 copy-done.1
  8.1 0.0 copy-done
  8.1 0.0 copy-done.2
  8.1 0.3 shard_map.68
  8.4 9.3 %collective-permute-start.2 = (f32[168,128]{1,0:T(8,128)S(1)}, f32[168,128]{1,0:T(8,128)S(1)}, u32[]{:S(2)}, u32[]{:S(2)}) collective-permute-start(f32[168,128]{1,0:T(8,128)S(1)} %get-tuple-element.18), channel_id=1, source_target_pairs={{0,1},{2,3},{4,5},{6,7},{8,9},{10,11},{12,13},{14,15},{1,0},{3,2},... | collective-permute-start | bytes 258056 | tf_op jit(solution)/shard_map/ppermute | solution.py:314
  17.7 1.9 %collective-permute-start.3 = (f32[168,128]{1,0:T(8,128)S(1)}, f32[168,128]{1,0:T(8,128)S(1)}, u32[]{:S(2)}, u32[]{:S(2)}) collective-permute-start(f32[168,128]{1,0:T(8,128)S(1)} %get-tuple-element.19), channel_id=1, source_target_pairs={{1,2},{3,4},{5,6},{7,8},{9,10},{11,12},{13,14},{2,1},{4,3},{6,5},{... | collective-permute-start | bytes 258056 | tf_op jit(solution)/shard_map/ppermute | solution.py:314
  19.7 0.0 collective-permute-done.2.side_one
  19.7 3.9 %collective-permute-done.3.side_two = f32[168,128]{1,0:T(8,128)S(1)} collective-permute-done((f32[168,128]{1,0:T(8,128)S(1)}, f32[168,128]{1,0:T(8,128)S(1)}, u32[]{:S(2)}, u32[]{:S(2)}) %collective-permute-start.3) | collective-permute-done | bytes 86048 | tf_op jit(solution)/shard_map/ppermute | solution.py:314
  23.5 2.0 %shard_map.69 = (f32[96,1024]{1,0:T(8,128)S(1)}, f32[128,128]{1,0:T(8,128)S(1)}) custom-call(f32[32,8,128]{2,1,0:T(8,128)S(1)} %copy-done, f32[32,8,128]{2,1,0:T(8,128)S(1)} %copy-done.1, f32[8,128]{1,0:T(8,128)S(1)} %copy-done.2, f32[104,128]{1,0:T(8,128)S(1)} %get-tuple-element.16.lo, f32[104,128]{1,0:T(8,128)S(1)} %get-tuple-element.17.hi, ...), custom_call_target="tpu_custom_call" | custom-call | tf_op jit(solution)/shard_map/pallas_call | solution.py:300
  25.5 10.6 %all_to_all.23 = f32[16,8,128]{2,1,0:T(8,128)S(1)} all-to-all(f32[16,8,128]{2,1,0:T(8,128)S(1)} %bitcast.5), channel_id=1, replica_groups=mesh['gx'=32,'gy'=16] {'gy'}, dimensions={0} | all-to-all | bytes 131072 | tf_op jit(solution)/shard_map/all_to_all | solution.py:318
  36.1 27.1 %all_to_all.24 = f32[32,8,128]{2,1,0:T(8,128)S(1)} all-to-all(f32[32,8,128]{2,1,0:T(8,128)S(1)} %tile.4), channel_id=1, replica_groups=mesh['gx'=32,'gy'=16] {'gx'}, dimensions={0} | all-to-all | bytes 262144 | tf_op jit(solution)/shard_map/all_to_all | solution.py:318
  63.2 0.0 copy-start.3
  63.2 11.8 %all_to_all.25 = f32[16,8,128]{2,1,0:T(8,128)S(1)} all-to-all(f32[16,8,128]{2,1,0:T(8,128)S(1)} %tile.5), channel_id=1, replica_groups=mesh['gx'=32,'gy'=16] {'gy'}, dimensions={0} | all-to-all | bytes 131072 | tf_op jit(solution)/shard_map/all_to_all | solution.py:318
  75.0 0.0 copy-done.3
  75.0 6.7 %shard_map.70 = (f32[32,8,128]{2,1,0:T(8,128)}, f32[32,8,128]{2,1,0:T(8,128)}, f32[1,32]{1,0:T(1,128)}) custom-call(f32[128,128]{1,0:T(8,128)S(1)} %bitcast.4, s32[32,96]{1,0:T(8,128)S(1)} %bitcast.6, f32[96,1024]{1,0:T(8,128)S(1)} %get-tuple-element.21.refs_2_), custom_call_target="tpu_custom_call" | custom-call | tf_op jit(solution)/shard_map/pallas_call | solution.py:300
  (4 shorter events, 0.1 us)
Async XLA Ops:
  0.6 7.5 %copy-start.1 = (f32[32,8,128]{2,1,0:T(8,128)S(1)}, f32[32,8,128]{2,1,0:T(8,128)}, u32[]{:S(2)}) copy-start(f32[32,8,128]{2,1,0:T(8,128)} %search.3) | copy-start | bytes 393220
  0.6 7.5 %copy-start = (f32[32,8,128]{2,1,0:T(8,128)S(1)}, f32[32,8,128]{2,1,0:T(8,128)}, u32[]{:S(2)}) copy-start(f32[32,8,128]{2,1,0:T(8,128)} %basis.3) | copy-start | bytes 393220
  0.7 7.5 %copy-start.2 = (f32[8,128]{1,0:T(8,128)S(1)}, f32[8,128]{1,0:T(8,128)}, u32[]{:S(2)}) copy-start(f32[8,128]{1,0:T(8,128)} %cond.3) | copy-start | bytes 12292
  2.4 5.7 %collective-permute-start = (f32[104,128]{1,0:T(8,128)}, f32[104,128]{1,0:T(8,128)S(1)}, u32[]{:S(2)}, u32[]{:S(2)}) collective-permute-start(f32[104,128]{1,0:T(8,128)} %get-tuple-element.14), channel_id=1, source_target_pairs={{0,16},{32,48},{64,80},{96,112},{128,144},{160,176},{192,208},{224... | collective-permute-start | bytes 159752 | tf_op jit(solution)/shard_map/ppermute | solution.py:314
  6.4 1.7 %collective-permute-start.1 = (f32[104,128]{1,0:T(8,128)}, f32[104,128]{1,0:T(8,128)S(1)}, u32[]{:S(2)}, u32[]{:S(2)}) collective-permute-start(f32[104,128]{1,0:T(8,128)} %get-tuple-element.15), channel_id=1, source_target_pairs={{16,32},{48,64},{80,96},{112,128},{144,160},{176,192},{208,224},{2... | collective-permute-start | bytes 159752 | tf_op jit(solution)/shard_map/ppermute | solution.py:314
  8.4 11.3 %collective-permute-start.2 = (f32[168,128]{1,0:T(8,128)S(1)}, f32[168,128]{1,0:T(8,128)S(1)}, u32[]{:S(2)}, u32[]{:S(2)}) collective-permute-start(f32[168,128]{1,0:T(8,128)S(1)} %get-tuple-element.18), channel_id=1, source_target_pairs={{0,1},{2,3},{4,5},{6,7},{8,9},{10,11},{12,13},{14,15},{1,0},{3,2},... | collective-permute-start | bytes 258056 | tf_op jit(solution)/shard_map/ppermute | solution.py:314
  17.7 5.8 %collective-permute-start.3 = (f32[168,128]{1,0:T(8,128)S(1)}, f32[168,128]{1,0:T(8,128)S(1)}, u32[]{:S(2)}, u32[]{:S(2)}) collective-permute-start(f32[168,128]{1,0:T(8,128)S(1)} %get-tuple-element.19), channel_id=1, source_target_pairs={{1,2},{3,4},{5,6},{7,8},{9,10},{11,12},{13,14},{2,1},{4,3},{6,5},{... | collective-permute-start | bytes 258056 | tf_op jit(solution)/shard_map/ppermute | solution.py:314
  63.2 11.8 %copy-start.3 = (s32[96,32]{0,1:T(8,128)S(1)}, s32[96,32]{0,1:T(8,128)}, u32[]{:S(2)}) copy-start(s32[96,32]{0,1:T(8,128)} %param.7) | copy-start | bytes 36868

commit v3 on v2

--- a/solution.py
+++ b/solution.py
@@ -65,40 +65,64 @@
     two[96:104, :] = cond[...]
 
 
-def pack_sides(basis, search, cond, row_one, row_two, side_one, side_two, lo, hi, right, left):
+def pack_layers(rows, right):
+    lane = lanes(rows[0].shape) // CZ
+    outer = second = None
+    for s in range(ROWS):
+        moved = roll(rows[s], CZ * (s + 1 if right else s))
+        at = (s - 1 if right else s + 1) % ROWS
+        outer = moved if outer is None else jnp.where(lane == s, moved, outer)
+        second = moved if second is None else jnp.where(lane == at, moved, second)
+    return outer, second
+
+
+def pack_ends(before, after, right):
+    before = roll(before, CZ if right else 0)
+    after = roll(after, 2 * CZ if right else CZ)
+    return jnp.where(lanes(before.shape) < CZ, before, after)
+
+
+def pack_sides(basis, search, cond, row_two, row_one, side_one, side_two, lo, hi, right, left):
     sort_sides("gx", row_one, row_two, lo, hi)
-    fields = [lo[32:64, :]] + [basis[:, s, :] for s in range(ROWS)] + [hi[0:32, :]]
-    fields += [search[:, s, :] for s in range(ROWS)]
-    conds = [lo[103:104, :]] + [cond[s : s + 1, :] for s in range(ROWS)] + [hi[96:97, :]]
-    for message, base in ((right, 32), (left, 0)):
-        for rows, start, step in ((fields, 0, 32), (conds, 160, 1)):
-            for tile in range((len(rows) + 3) // 4):
-                packed = None
-                for k, row in enumerate(rows[4 * tile : 4 * tile + 4]):
-                    if step == 1:
-                        row = jnp.broadcast_to(row, (8, LANES))
-                    moved = roll(row, base + 32 * k)
-                    if packed is None:
-                        packed = moved
-                    else:
-                        packed = jnp.where(lanes(moved.shape) >= 32 * k, moved, packed)
-                message[start + step * tile : start + step * (tile + 1), :] = packed[:step]
-        message[163:168, :] = jnp.zeros((5, LANES), jnp.float32)
+    block = (8, LANES)
+    field = [basis[:, s, :] for s in range(ROWS)]
+    other = [search[:, s, :] for s in range(ROWS)]
+    cells = [jnp.broadcast_to(cond[s : s + 1, :], block) for s in range(ROWS)]
+    cell_lo = jnp.broadcast_to(lo[103:104, :], block)
+    cell_hi = jnp.broadcast_to(hi[96:97, :], block)
+    lane = lanes(block)
+    for message, to_right in ((right, True), (left, False)):
+        message[0:32, :], message[32:64, :] = pack_layers(field, to_right)
+        message[64:96, :] = pack_layers(other, to_right)[0]
+        ends = pack_ends(lo[32:64, :], hi[0:32, :], to_right)
+        folded = ends[0:8]
+        for q in range(1, 4):
+            folded = jnp.where(lane >= 32 * q, roll(ends[8 * q : 8 * q + 8], 32 * q), folded)
+        message[96:104, :] = folded
+        cell_outer, cell_second = pack_layers(cells, to_right)
+        message[104:105, :] = cell_outer[:1]
+        message[105:106, :] = cell_second[:1]
+        message[106:107, :] = pack_ends(cell_lo, cell_hi, to_right)[:1]
+        message[107:112, :] = jnp.zeros((5, LANES), jnp.float32)
     sort_sides("gy", left, right, side_one, side_two)
 
 
-def side_tile(low, high, index, start, step):
-    tile, k = divmod(index, 4)
-    place = start + step * tile
-    below = low[place : place + step, :]
-    above = high[place : place + step, :]
-    if step == 1:
-        below = jnp.broadcast_to(below, (8, LANES))
-        above = jnp.broadcast_to(above, (8, LANES))
-    lane = lanes(below.shape)
-    below = roll(below, 96 - 32 * k)
-    above = roll(above, -32 * k)
-    return jnp.where(lane >= 96, below, jnp.where(lane < 32, above, 0.0))
+def side_tile(low, high, s):
+    lane = lanes(low[0].shape) // CZ
+    if 0 <= s < ROWS:
+        above = [roll(part, -CZ * s) for part in high[:2]]
+        below = [roll(part, CZ * (7 - s)) for part in low[:2]]
+        tile = jnp.where(lane == 0, above[0], jnp.where(lane == 7, below[0], 0.0))
+        if len(above) == 2:
+            tile = jnp.where(lane == 1, above[1], jnp.where(lane == 6, below[1], tile))
+        return tile
+    k = 0 if s < 0 else 1
+    above, below = roll(high[2], -CZ * k), roll(low[2], CZ * (7 - k))
+    return jnp.where(lane == 0, above, jnp.where(lane == 7, below, 0.0))
+
+
+def unfolded(folded):
+    return jnp.concatenate([roll(folded, -32 * q) for q in range(4)], 0)
 
 
 def next_y(own, side):
@@ -122,15 +146,20 @@
 
 
 def images(
-    basis, search, cond, lo, hi, side_one, side_two, fields, sums, conds, coef, image, stack, low, high
+    basis, search, cond, lo, hi, side_two, side_one, fields, sums, conds, coef, image, stack, low, high
 ):
     sort_sides("gy", side_one, side_two, low, high)
+    basis_sides = [(part[0:32, :], part[32:64, :], unfolded(part[96:104, :])) for part in (low, high)]
+    search_sides = [(part[64:96, :],) for part in (low, high)]
+    cond_sides = [
+        [jnp.broadcast_to(part[r : r + 1, :], (8, LANES)) for r in range(104, 107)] for part in (low, high)
+    ]
     conds[...] = jnp.zeros_like(conds)
     conds[0, 0:2, :] = lo[102:104, :]
     conds[0, 2:10, :] = cond[...]
     conds[0, 10:12, :] = hi[96:98, :]
     for r in range(10):
-        conds[1, r + 1 : r + 2, :] = side_tile(low, high, r, 160, 1)[:1]
+        conds[1, r + 1 : r + 2, :] = side_tile(*cond_sides, r - 1)[:1]
     cond_a, cond_b = conds[0, 0:16, :], conds[1, 0:16, :]
     after = next_y(cond_a, cond_b)
     before = prev_y(cond_a, cond_b)
@@ -165,10 +194,10 @@
     def valid(part, r, array):
         return jnp.where(conds[part, r + 2 : r + 3, :] > 0.0, array, 0.0)
 
-    sides = {r: side_tile(low, high, r + 1, 0, 32) for r in range(-1, 2)}
+    sides = {r: side_tile(*basis_sides, r) for r in range(-1, 2)}
     for r in range(-1, ROWS + 1):
         if 1 <= r < ROWS:
-            sides[r + 1] = side_tile(low, high, r + 2, 0, 32)
+            sides[r + 1] = side_tile(*basis_sides, r + 1)
         own = basis_row(r)
         pairs = beside(own, sides[r])
         first = operator(0, r, own, pairs[0], basis_row(r - 1), basis_row(r + 1))
@@ -180,7 +209,7 @@
     for s in range(ROWS):
         at = slice(LANES * s, LANES * (s + 1))
         field = search[:, s, :]
-        pairs = beside(field, side_tile(low, high, 10 + s, 0, 32))
+        pairs = beside(field, side_tile(*search_sides, s))
         x_low = lo[64:96, :] if s == 0 else search[:, s - 1, :]
         x_high = hi[64:96, :] if s == ROWS - 1 else search[:, s + 1, :]
         stack[128:160, at] = operator(0, s, field, pairs[0], x_low, x_high)
@@ -195,48 +224,70 @@
         fields[64:96, at] = field
 
     product = dot_nt(stack[0:96, :], stack[...])
-    last = product[64:96, 128:160]
-    sums[0:32, :] = jnp.concatenate([product[0:32, 0:96], last], 1)
-    sums[32:64, :] = jnp.concatenate([product[64:96, 96:128], product[32:64, 32:128]], 1)
-    corner = product[64:96, 64:96]
-    sums[64:72, :] = jnp.concatenate([corner[8 * k : 8 * k + 8] for k in range(4)], 1)
-    sums[72:128, :] = jnp.zeros((56, LANES), jnp.float32)
+    blocks = [[product[32 * i : 32 * i + 32, 32 * j : 32 * j + 32] for j in range(5)] for i in range(3)]
+    lower = lanes((32, 32)) <= lax.broadcasted_iota(jnp.int32, (32, 32), 0)
+    first = jnp.where(lower, blocks[0][0], blocks[2][2])
+    second = jnp.where(lower, blocks[1][1], blocks[2][4])
+    sums[0:32, :] = jnp.concatenate([first, blocks[0][1], blocks[0][2], blocks[2][3]], 1)
+    for k, block in enumerate((second, blocks[1][2], blocks[1][3])):
+        pieces = [block[8 * q : 8 * q + 8] for q in range(4)]
+        sums[32 + 8 * k : 40 + 8 * k, :] = jnp.concatenate(pieces, 1)
+    rest = jnp.zeros((1, 64), jnp.float32)
+    sums[56:57, :] = jnp.concatenate([diagonal(blocks[2][2]), diagonal(blocks[2][4]), rest], 1)
+    sums[57:64, :] = jnp.zeros((7, LANES), jnp.float32)
+
+
+def diagonal(block):
+    here = lanes((32, 32)) == lax.broadcasted_iota(jnp.int32, (32, 32), 0)
+    return jnp.sum(jnp.where(here, block, 0.0), 0, keepdims=True)
+
+
+def parted(mixed, ends):
+    turned = mixed.T
+    lane = lanes((32, 32))
+    row = lax.broadcasted_iota(jnp.int32, (32, 32), 0)
+    upper = jnp.where(lane > row, mixed, turned)
+    return jnp.where(lane <= row, mixed, turned), jnp.where(lane == row, ends, upper)
 
 
 def eliminate(slabs):
     slabs = list(slabs)
     count = len(slabs)
-    lane = lanes((8, LANES))
-    row = lax.broadcasted_iota(jnp.int32, (8, LANES), 0)
+    tile = (8, LANES)
+    lane = lanes(tile)
+    row = lax.broadcasted_iota(jnp.int32, tile, 0)
     width = 4
     for start in range(0, 8 * count, width):
-        g = start // 8
+        g, at = divmod(start, 8)
         cols = [
-            {i: jnp.broadcast_to(slabs[i][:, start + k : start + k + 1], (8, LANES)) for i in range(g, count)}
+            [jnp.broadcast_to(slab[:, start + k : start + k + 1], tile) for slab in slabs[g:]]
             for k in range(width)
         ]
+        block = [
+            [jnp.broadcast_to(cols[k][0][at + m : at + m + 1, :], tile) for k in range(m + 1)]
+            for m in range(width)
+        ]
+        rows = [jnp.broadcast_to(slabs[g][at + m : at + m + 1, :], tile) for m in range(width)]
         for k in range(width):
-            j = start + k
-            at = j % 8
-            pivot = cols[k][g][at : at + 1, :]
-            inverse = 1.0 / pivot
-            root = lax.rsqrt(pivot)
-            here = lane[:1] == j
-            pivot_row = jnp.where(here, 1.0, slabs[g][at : at + 1, :])
-            scaled = pivot_row * inverse
-            later = [cols[m][g][at : at + 1, :] * inverse for m in range(k + 1, width)]
-            for i in range(g, count):
+            here = lane == start + k
+            root = lax.rsqrt(block[k][k])
+            inverse = root * root
+            scaled = jnp.where(here, 1.0, rows[k]) * inverse
+            rows[k] = jnp.where(here, 1.0, rows[k]) * root
+            column = [block[m][k] for m in range(width)[k + 1 :]]
+            later = [entry * inverse for entry in column]
+            for m in range(k + 1, width):
+                rows[m] = jnp.where(here, 0.0, rows[m]) - column[m - k - 1] * scaled
+                for n in range(k + 1, m + 1):
+                    block[m][n] = block[m][n] - (column[m - k - 1] * column[n - k - 1]) * inverse
+            for i in range(len(cols[k])):
                 factor = cols[k][i]
-                kept = jnp.where(lane == j, 0.0, slabs[i])
-                if i == g:
-                    factor = jnp.where(row > at, factor, 0.0)
-                    kept = jnp.where(row > at, kept, slabs[i])
-                    fresh = kept - factor * scaled
-                    slabs[i] = jnp.where(row == at, pivot_row * root, fresh)
-                else:
-                    slabs[i] = kept - factor * scaled
+                fresh = jnp.where(here, 0.0, slabs[g + i]) - factor * scaled
+                slabs[g + i] = jnp.where(row >= at + width, fresh, slabs[g]) if i == 0 else fresh
                 for m in range(k + 1, width):
                     cols[m][i] = cols[m][i] - factor * later[m - k - 1]
+        for k in range(width):
+            slabs[g] = jnp.where(row == at + k, rows[k], slabs[g])
     return slabs
 
 
@@ -249,10 +300,13 @@
 def update(scale, sums, start, fields, new_basis, new_search, values):
     first = sums[0:32, :] * scale
     second = sums[32:64, :] * scale
-    third = sums[64:72, :] * scale
-    xx, xy, xp, pr = (first[:, 32 * k : 32 * k + 32] for k in range(4))
-    pz, yy, yp, yz = (second[:, 32 * k : 32 * k + 32] for k in range(4))
-    pp = jnp.concatenate([third[:, 32 * k : 32 * k + 32] for k in range(4)], 0)
+    mixed, xy, xp, pz = (first[:, 32 * k : 32 * k + 32] for k in range(4))
+    other, yp, yz = (
+        jnp.concatenate([second[8 * k : 8 * k + 8, 32 * q : 32 * q + 32] for q in range(4)], 0)
+        for k in range(3)
+    )
+    xx, pp = parted(mixed, second[24:25, 0:32])
+    yy, pr = parted(other, second[24:25, 32:64])
     px, py, zp = xp.T, yp.T, pz.T
     zero = jnp.zeros((32, 32), jnp.float32)
     gram = [
@@ -271,31 +325,30 @@
     lower_inv = lower_part(
         eliminate([block[8 * k : 8 * k + 8] for block in gram for k in range(4)]), 96
     )
-    ritz = dot_nt(dot_nn(lower_inv, projected), lower_inv)
-    ritz = 0.5 * (ritz + ritz.T)
+    half = dot_nn(lower_inv, projected)
+    ritz = 0.5 * (dot_nt(half, lower_inv) + dot_nt(lower_inv, half))
     bound = jnp.max(jnp.sum(jnp.abs(ritz), 0, keepdims=True), 1, keepdims=True)
     seed = start[...].astype(jnp.float32)
     moved = bound * seed - dot_nn(seed, ritz)
     square = jnp.concatenate([dot_nt(moved, moved), jnp.zeros((32, 96), jnp.float32)], 1)
-    small_inv = lower_part(eliminate([square[8 * k : 8 * k + 8] for k in range(4)]), 32)
-    coeffs = dot_nn(small_inv, moved)
-    weights = dot_nn(coeffs, lower_inv)
-    terms = coeffs * dot_nn(coeffs, ritz)
-    values[...] = dot_nt(jnp.ones((8, 96), jnp.float32), terms)[0:1, :]
-    diagonal = lanes((32, 32)) == lax.broadcasted_iota(jnp.int32, (32, 32), 0)
-    along = jnp.sum(jnp.where(diagonal, xy, 0.0), 0, keepdims=True)
-    norms = jnp.sum(jnp.where(diagonal, xx, 0.0), 0, keepdims=True)
-    quotient = along / norms
+    weights = dot_nn(moved, lower_inv)
+    quotient = diagonal(xy) / diagonal(xx)
     middle = weights[:, 32:64]
     search_weights = jnp.concatenate([-(middle * quotient), middle, weights[:, 64:96]], 1)
-    both = jnp.concatenate([weights, search_weights], 0)
-    result = dot_nn(both, fields[...])
+    mixed_fields = dot_nn(jnp.concatenate([weights, search_weights], 0), fields[...])
+    mixed_ritz = dot_nn(moved, ritz)
+    small_inv = lower_part(eliminate([square[8 * k : 8 * k + 8] for k in range(4)]), 32)
+    both = jnp.concatenate([mixed_fields[0:32], mixed_fields[32:64]], 1)
+    result = dot_nn(small_inv, both)
+    terms = dot_nn(small_inv, moved) * dot_nn(small_inv, mixed_ritz)
+    values[...] = dot_nt(jnp.ones((8, 96), jnp.float32), terms)[0:1, :]
+    wide = ROWS * LANES
     for s in range(ROWS):
-        new_basis[:, s, :] = result[0:32, LANES * s : LANES * (s + 1)]
-        new_search[:, s, :] = result[32:64, LANES * s : LANES * (s + 1)]
-
-
-def call(kernel, outs, *args, scratch=(), place=VMEM, room=32):
+        new_basis[:, s, :] = result[:, LANES * s : LANES * (s + 1)]
+        new_search[:, s, :] = result[:, wide + LANES * s : wide + LANES * (s + 1)]
+
+
+def call(kernel, outs, *args, scratch=(), place=VMEM):
     shapes = [jax.ShapeDtypeStruct(shape, jnp.float32) for shape in outs]
     return pl.pallas_call(
         kernel,
@@ -305,7 +358,7 @@
         scratch_shapes=[
             pltpu.VMEM(shape, jnp.float32) if isinstance(shape, tuple) else shape for shape in scratch
         ],
-        compiler_params=pltpu.CompilerParams(vmem_limit_bytes=room * 1024 * 1024),
+        compiler_params=pltpu.CompilerParams(vmem_limit_bytes=32 * 1024 * 1024),
     )(*args)
 
 
@@ -336,36 +389,36 @@
     rows = call(
         pack_rows,
         [(104, LANES)] * 2,
+        *(pltpu.with_memory_space_constraint(x, pltpu.HBM) for x in (basis, search, conductivity)),
+        scratch=blocks + [pltpu.SemaphoreType.DMA((3,))],
+        place=pl.BlockSpec(memory_space=pltpu.HBM),
+    )
+    row_two = paired(rows[1], "gx", 1)
+    row_one = paired(rows[0], "gx", 0)
+    side_one, side_two, lo, hi = call(
+        pack_sides,
+        [(112, LANES)] * 2 + [(104, LANES)] * 2,
         basis,
         search,
         conductivity,
-        scratch=blocks + [pltpu.SemaphoreType.DMA((3,))],
-        place=pl.BlockSpec(memory_space=pl.ANY),
-        room=63,
-    )
-    rows = [paired(rows[k], "gx", k) for k in range(2)]
-    side_one, side_two, lo, hi = call(
-        pack_sides,
-        [(168, LANES)] * 2 + [(104, LANES)] * 2,
-        basis,
-        search,
-        conductivity,
-        *rows,
-        scratch=[(168, LANES)] * 2,
-    )
-    side_one, side_two = paired(side_one, "gy", 0), paired(side_two, "gy", 1)
+        row_two,
+        row_one,
+        scratch=[(112, LANES)] * 2,
+    )
+    side_two = paired(side_two, "gy", 1)
+    side_one = paired(side_one, "gy", 0)
     fields, sums = call(
         images,
-        [(96, ROWS * LANES), (LANES, LANES)],
+        [(96, ROWS * LANES), (64, LANES)],
         basis,
         search,
         conductivity,
         lo,
         hi,
+        side_two,
         side_one,
-        side_two,
         scratch=[(2, 24, LANES), (2, 5, 16, LANES), (2, 10, MODES, LANES), (160, ROWS * LANES)]
-        + [(168, LANES)] * 2,
+        + [(112, LANES)] * 2,
     )
     sums = total(sums)
 

time: 82.1 us -> 77.6 us (0.945)
  waiting for transfers between devices: 4.92 us -> 2.36 us
  blocking collectives: 49.4 us -> 47.7 us
  starting transfers between devices: 15.9 us -> 14.6 us
  Pallas kernels: 10.7 us -> 11.7 us
    ppermute x4, waiting for transfers between devices: 4.92 us -> 2.36 us  [paired(): return lax.ppermute(array, axis, pairs + [(j, i) for i, j in pairs])]
    all_to_all x3, blocking collectives: 49.4 us -> 47.7 us  [exchanged(): return lax.all_to_all(array, axis, 0, 0, tiled=True)]
    ppermute x4, starting transfers between devices: 15.9 us -> 14.6 us  [paired(): return lax.ppermute(array, axis, pairs + [(j, i) for i, j in pairs])]
    pallas_call x4, Pallas kernels: 10.7 us -> 11.7 us  [call(): pl.pallas_call(kernel, out_shape=shapes, in_specs=[place] * len(args), ou...]
where the time goes in v3:
time: 77.6 us; the launch traced here: 77.3 us
  blocking collectives  47.7 us (61%)
  starting transfers between devices  14.6 us (19%)
  Pallas kernels  11.7 us (15%)
  waiting for transfers between devices  2.36 us (3%)
    all_to_all x3, blocking collectives, exchanged(): return lax.all_to_all(array, axis, 0, 0, tiled=True)  47.7 us
    ppermute x4, starting transfers between devices, paired(): return lax.ppermute(array, axis, pairs + [(j, i) for i, j in pairs])  14.6 us
    pallas_call x4, Pallas kernels, call(): pl.pallas_call(kernel, out_shape=shapes, in_specs=[place] * len(args), ou...  11.7 us
    ppermute x4, waiting for transfers between devices, paired(): return lax.ppermute(array, axis, pairs + [(j, i) for i, j in pairs])  2.36 us
  transfers between devices with their start and end apart: 4, of which 2 were waited for; matrix products, arithmetic and copies ran while one was open for 0% of the time, Pallas kernels for 0%

profile of v3, /device:TPU:1, one launch (start us, length us, event | category | flops | bytes accessed | tf_op | source)
XLA Modules:
  0.0 77.3 jit_solution(15874758330640674051)
XLA Ops:
  0.6 0.0 copy-start.1
  0.6 0.0 copy-start
  0.7 0.0 copy-start.2
  0.7 1.1 %shard_map.67 = (f32[104,128]{1,0:T(8,128)S(1)}, f32[104,128]{1,0:T(8,128)S(1)}) custom-call(f32[32,8,128]{2,1,0:T(8,128)} %basis.3, f32[32,8,128]{2,1,0:T(8,128)} %search.3, f32[8,128]{1,0:T(8,128)} %cond.3), custom_call_target="tpu_custom_call" | custom-call | tf_op jit(solution)/shard_map/pallas_call | solution.py:353
  1.8 0.7 collective-permute-start
  2.5 6.4 %collective-permute-start.1 = (f32[104,128]{1,0:T(8,128)S(1)}, f32[104,128]{1,0:T(8,128)S(1)}, u32[]{:S(2)}, u32[]{:S(2)}) collective-permute-start(f32[104,128]{1,0:T(8,128)S(1)} %get-tuple-element.15), channel_id=1, source_target_pairs={{0,16},{32,48},{64,80},{96,112},{128,144},{160,176},{192,208},{224... | collective-permute-start | bytes 159752 | tf_op jit(solution)/shard_map/ppermute | solution.py:367
  8.9 0.0 collective-permute-done.row_two
  8.9 1.5 %collective-permute-done.1.row_one = f32[104,128]{1,0:T(8,128)S(1)} collective-permute-done((f32[104,128]{1,0:T(8,128)S(1)}, f32[104,128]{1,0:T(8,128)S(1)}, u32[]{:S(2)}, u32[]{:S(2)}) %collective-permute-start.1) | collective-permute-done | bytes 53280 | tf_op jit(solution)/shard_map/ppermute | solution.py:367
  10.4 0.0 copy-done.1
  10.4 0.0 copy-done
  10.4 0.0 copy-done.2
  10.4 0.4 shard_map.68
  10.8 4.9 %collective-permute-start.2 = (f32[112,128]{1,0:T(8,128)S(1)}, f32[112,128]{1,0:T(8,128)S(1)}, u32[]{:S(2)}, u32[]{:S(2)}) collective-permute-start(f32[112,128]{1,0:T(8,128)S(1)} %get-tuple-element.18), channel_id=1, source_target_pairs={{1,2},{3,4},{5,6},{7,8},{9,10},{11,12},{13,14},{2,1},{4,3},{6,5},{... | collective-permute-start | bytes 172040 | tf_op jit(solution)/shard_map/ppermute | solution.py:367
  15.7 2.6 %collective-permute-start.3 = (f32[112,128]{1,0:T(8,128)S(1)}, f32[112,128]{1,0:T(8,128)S(1)}, u32[]{:S(2)}, u32[]{:S(2)}) collective-permute-start(f32[112,128]{1,0:T(8,128)S(1)} %get-tuple-element.19), channel_id=1, source_target_pairs={{0,1},{2,3},{4,5},{6,7},{8,9},{10,11},{12,13},{14,15},{1,0},{3,2},... | collective-permute-start | bytes 172040 | tf_op jit(solution)/shard_map/ppermute | solution.py:367
  18.3 0.0 collective-permute-done.2.side_two
  18.3 0.9 %collective-permute-done.3.side_one = f32[112,128]{1,0:T(8,128)S(1)} collective-permute-done((f32[112,128]{1,0:T(8,128)S(1)}, f32[112,128]{1,0:T(8,128)S(1)}, u32[]{:S(2)}, u32[]{:S(2)}) %collective-permute-start.3) | collective-permute-done | bytes 57376 | tf_op jit(solution)/shard_map/ppermute | solution.py:367
  19.2 2.2 %shard_map.69 = (f32[96,1024]{1,0:T(8,128)S(1)}, f32[64,128]{1,0:T(8,128)S(1)}) custom-call(f32[32,8,128]{2,1,0:T(8,128)S(1)} %copy-done, f32[32,8,128]{2,1,0:T(8,128)S(1)} %copy-done.1, f32[8,128]{1,0:T(8,128)S(1)} %copy-done.2, f32[104,128]{1,0:T(8,128)S(1)} %get-tuple-element.16.lo, f32[104,128]{1,0:T(8,128)S(1)} %get-tuple-element.17.hi, ...), custom_call_target="tpu_custom_call" | custom-call | tf_op jit(solution)/shard_map/pallas_call | solution.py:353
  21.4 14.4 %all_to_all.23 = f32[16,4,128]{2,1,0:T(4,128)S(1)} all-to-all(f32[16,4,128]{2,1,0:T(4,128)S(1)} %bitcast.5), channel_id=1, replica_groups=mesh['gx'=32,'gy'=16] {'gy'}, dimensions={0} | all-to-all | bytes 65536 | tf_op jit(solution)/shard_map/all_to_all | solution.py:371
  35.8 21.6 %all_to_all.24 = f32[32,4,128]{2,1,0:T(4,128)S(1)} all-to-all(f32[32,4,128]{2,1,0:T(4,128)S(1)} %tile.4), channel_id=1, replica_groups=mesh['gx'=32,'gy'=16] {'gx'}, dimensions={0} | all-to-all | bytes 131072 | tf_op jit(solution)/shard_map/all_to_all | solution.py:371
  57.5 0.0 copy-start.3
  57.5 11.7 %all_to_all.25 = f32[16,4,128]{2,1,0:T(4,128)S(1)} all-to-all(f32[16,4,128]{2,1,0:T(4,128)S(1)} %tile.5), channel_id=1, replica_groups=mesh['gx'=32,'gy'=16] {'gy'}, dimensions={0} | all-to-all | bytes 65536 | tf_op jit(solution)/shard_map/all_to_all | solution.py:371
  69.2 0.0 copy-done.3
  69.2 8.1 %shard_map.70 = (f32[32,8,128]{2,1,0:T(8,128)}, f32[32,8,128]{2,1,0:T(8,128)}, f32[1,32]{1,0:T(1,128)}) custom-call(f32[64,128]{1,0:T(8,128)S(1)} %bitcast.4, s32[32,96]{1,0:T(8,128)S(1)} %bitcast.6, f32[96,1024]{1,0:T(8,128)S(1)} %get-tuple-element.21.refs_2_), custom_call_target="tpu_custom_call" | custom-call | tf_op jit(solution)/shard_map/pallas_call | solution.py:353
  (4 shorter events, 0.1 us)
Async XLA Ops:
  0.6 9.8 %copy-start.1 = (f32[32,8,128]{2,1,0:T(8,128)S(1)}, f32[32,8,128]{2,1,0:T(8,128)}, u32[]{:S(2)}) copy-start(f32[32,8,128]{2,1,0:T(8,128)} %search.3) | copy-start | bytes 393220
  0.6 9.8 %copy-start = (f32[32,8,128]{2,1,0:T(8,128)S(1)}, f32[32,8,128]{2,1,0:T(8,128)}, u32[]{:S(2)}) copy-start(f32[32,8,128]{2,1,0:T(8,128)} %basis.3) | copy-start | bytes 393220
  0.7 9.7 %copy-start.2 = (f32[8,128]{1,0:T(8,128)S(1)}, f32[8,128]{1,0:T(8,128)}, u32[]{:S(2)}) copy-start(f32[8,128]{1,0:T(8,128)} %cond.3) | copy-start | bytes 12292
  1.8 7.1 %collective-permute-start = (f32[104,128]{1,0:T(8,128)S(1)}, f32[104,128]{1,0:T(8,128)S(1)}, u32[]{:S(2)}, u32[]{:S(2)}) collective-permute-start(f32[104,128]{1,0:T(8,128)S(1)} %get-tuple-element.14), channel_id=1, source_target_pairs={{16,32},{48,64},{80,96},{112,128},{144,160},{176,192},{208,224},{2... | collective-permute-start | bytes 159752 | tf_op jit(solution)/shard_map/ppermute | solution.py:367
  2.5 7.9 %collective-permute-start.1 = (f32[104,128]{1,0:T(8,128)S(1)}, f32[104,128]{1,0:T(8,128)S(1)}, u32[]{:S(2)}, u32[]{:S(2)}) collective-permute-start(f32[104,128]{1,0:T(8,128)S(1)} %get-tuple-element.15), channel_id=1, source_target_pairs={{0,16},{32,48},{64,80},{96,112},{128,144},{160,176},{192,208},{224... | collective-permute-start | bytes 159752 | tf_op jit(solution)/shard_map/ppermute | solution.py:367
  10.8 7.6 %collective-permute-start.2 = (f32[112,128]{1,0:T(8,128)S(1)}, f32[112,128]{1,0:T(8,128)S(1)}, u32[]{:S(2)}, u32[]{:S(2)}) collective-permute-start(f32[112,128]{1,0:T(8,128)S(1)} %get-tuple-element.18), channel_id=1, source_target_pairs={{1,2},{3,4},{5,6},{7,8},{9,10},{11,12},{13,14},{2,1},{4,3},{6,5},{... | collective-permute-start | bytes 172040 | tf_op jit(solution)/shard_map/ppermute | solution.py:367
  15.7 3.5 %collective-permute-start.3 = (f32[112,128]{1,0:T(8,128)S(1)}, f32[112,128]{1,0:T(8,128)S(1)}, u32[]{:S(2)}, u32[]{:S(2)}) collective-permute-start(f32[112,128]{1,0:T(8,128)S(1)} %get-tuple-element.19), channel_id=1, source_target_pairs={{0,1},{2,3},{4,5},{6,7},{8,9},{10,11},{12,13},{14,15},{1,0},{3,2},... | collective-permute-start | bytes 172040 | tf_op jit(solution)/shard_map/ppermute | solution.py:367
  57.5 11.7 %copy-start.3 = (s32[96,32]{0,1:T(8,128)S(1)}, s32[96,32]{0,1:T(8,128)}, u32[]{:S(2)}) copy-start(s32[96,32]{0,1:T(8,128)} %param.7) | copy-start | bytes 36868

commit v4 on v3

--- a/solution.py
+++ b/solution.py
@@ -145,8 +145,33 @@
     return jnp.where(lanes(array.shape) % CZ == 0, roll(array, 1 - CZ), roll(array, 1))
 
 
+def inner(basis, search, cond, image, other, coef):
+    lane = lanes((ROWS, LANES))
+    cells = cond[...]
+    after, before = roll(cells, -CZ), roll(cells, CZ)
+    coef[0] = jnp.where(lane < LANES - CZ, 0.5 * (cells + after), 0.0)
+    coef[1] = jnp.where(lane >= CZ, 0.5 * (cells + before), 0.0)
+    coef[2] = 0.5 * (cells + next_z(cells))
+    coef[3] = 0.5 * (cells + prev_z(cells))
+    for field, result in ((basis, image), (search, other)):
+        flux = None
+        for s in range(ROWS):
+            own = field[:, s, :]
+            total = coef[0, s : s + 1, :] * (own - roll(own, -CZ))
+            total += coef[1, s : s + 1, :] * (own - roll(own, CZ))
+            total += coef[2, s : s + 1, :] * (own - next_z(own))
+            total += coef[3, s : s + 1, :] * (own - prev_z(own))
+            if s > 0:
+                total += flux
+            if s < ROWS - 1:
+                face = 0.5 * (cond[s : s + 1, :] + cond[s + 1 : s + 2, :])
+                flux = face * (field[:, s + 1, :] - own)
+                total -= flux
+            result[s] = total
+
+
 def images(
-    basis, search, cond, lo, hi, side_two, side_one, fields, sums, conds, coef, image, stack, low, high
+    basis, search, cond, inner_x, inner_p, lo, hi, side_two, side_one, fields, sums, conds, coef, image, stack, low, high
 ):
     sort_sides("gy", side_one, side_two, low, high)
     basis_sides = [(part[0:32, :], part[32:64, :], unfolded(part[96:104, :])) for part in (low, high)]
@@ -180,6 +205,20 @@
         total += coef[part, 4, i : i + 1, :] * (own - prev_z(own))
         return total
 
+    def outer(s, own, side, x_low, x_high):
+        i = s + 2
+        group = lanes(own.shape) // CZ
+        other = jnp.where(group == 0, roll(side, CZ), roll(side, -CZ))
+        first = lanes((1, LANES)) // CZ
+        face = jnp.where(first == 0, coef[0, 2, i : i + 1, :], 0.0)
+        face = jnp.where(first == 7, coef[0, 1, i : i + 1, :], face)
+        total = face * (own - other)
+        if s == 0:
+            total += coef[0, 0, i - 1 : i, :] * (own - x_low)
+        if s == ROWS - 1:
+            total += coef[0, 0, i : i + 1, :] * (own - x_high)
+        return total
+
     def beside(own, side):
         after, before = next_y(own, side), prev_y(own, side)
         return ((after[0], before[0]), (after[1], before[1]))
@@ -200,8 +239,11 @@
             sides[r + 1] = side_tile(*basis_sides, r + 1)
         own = basis_row(r)
         pairs = beside(own, sides[r])
-        first = operator(0, r, own, pairs[0], basis_row(r - 1), basis_row(r + 1))
-        image[0, r + 1] = first if 0 <= r < ROWS else valid(0, r, first)
+        if 0 <= r < ROWS:
+            image[0, r + 1] = inner_x[r] + outer(r, own, sides[r], basis_row(-1), basis_row(ROWS))
+        else:
+            first = operator(0, r, own, pairs[0], basis_row(r - 1), basis_row(r + 1))
+            image[0, r + 1] = valid(0, r, first)
         if 0 <= r < ROWS:
             second = operator(1, r, sides[r], pairs[1], sides[r - 1], sides[r + 1])
             image[1, r + 1] = valid(1, r, second)
@@ -209,10 +251,8 @@
     for s in range(ROWS):
         at = slice(LANES * s, LANES * (s + 1))
         field = search[:, s, :]
-        pairs = beside(field, side_tile(*search_sides, s))
-        x_low = lo[64:96, :] if s == 0 else search[:, s - 1, :]
-        x_high = hi[64:96, :] if s == ROWS - 1 else search[:, s + 1, :]
-        stack[128:160, at] = operator(0, s, field, pairs[0], x_low, x_high)
+        side = side_tile(*search_sides, s)
+        stack[128:160, at] = inner_p[s] + outer(s, field, side, lo[64:96, :], hi[64:96, :])
         own = image[0, s + 1]
         pairs = beside(own, image[1, s + 1])
         stack[96:128, at] = operator(0, s, own, pairs[0], image[0, s], image[0, s + 2])
@@ -253,41 +293,37 @@
 def eliminate(slabs):
     slabs = list(slabs)
     count = len(slabs)
-    tile = (8, LANES)
-    lane = lanes(tile)
-    row = lax.broadcasted_iota(jnp.int32, tile, 0)
+    lane = lanes((8, LANES))
+    row = lax.broadcasted_iota(jnp.int32, (8, LANES), 0)
     width = 4
     for start in range(0, 8 * count, width):
-        g, at = divmod(start, 8)
+        g = start // 8
         cols = [
-            [jnp.broadcast_to(slab[:, start + k : start + k + 1], tile) for slab in slabs[g:]]
+            {i: jnp.broadcast_to(slabs[i][:, start + k : start + k + 1], (8, LANES)) for i in range(g, count)}
             for k in range(width)
         ]
-        block = [
-            [jnp.broadcast_to(cols[k][0][at + m : at + m + 1, :], tile) for k in range(m + 1)]
-            for m in range(width)
-        ]
-        rows = [jnp.broadcast_to(slabs[g][at + m : at + m + 1, :], tile) for m in range(width)]
         for k in range(width):
-            here = lane == start + k
-            root = lax.rsqrt(block[k][k])
+            j = start + k
+            at = j % 8
+            pivot = cols[k][g][at : at + 1, :]
+            root = lax.rsqrt(pivot)
             inverse = root * root
-            scaled = jnp.where(here, 1.0, rows[k]) * inverse
-            rows[k] = jnp.where(here, 1.0, rows[k]) * root
-            column = [block[m][k] for m in range(width)[k + 1 :]]
-            later = [entry * inverse for entry in column]
-            for m in range(k + 1, width):
-                rows[m] = jnp.where(here, 0.0, rows[m]) - column[m - k - 1] * scaled
-                for n in range(k + 1, m + 1):
-                    block[m][n] = block[m][n] - (column[m - k - 1] * column[n - k - 1]) * inverse
-            for i in range(len(cols[k])):
+            here = lane[:1] == j
+            pivot_row = jnp.where(here, 1.0, slabs[g][at : at + 1, :])
+            scaled = pivot_row * inverse
+            later = [cols[m][g][at : at + 1, :] * inverse for m in range(k + 1, width)]
+            for i in range(g, count):
                 factor = cols[k][i]
-                fresh = jnp.where(here, 0.0, slabs[g + i]) - factor * scaled
-                slabs[g + i] = jnp.where(row >= at + width, fresh, slabs[g]) if i == 0 else fresh
+                kept = jnp.where(lane == j, 0.0, slabs[i])
+                if i == g:
+                    factor = jnp.where(row > at, factor, 0.0)
+                    kept = jnp.where(row > at, kept, slabs[i])
+                    fresh = kept - factor * scaled
+                    slabs[i] = jnp.where(row == at, pivot_row * root, fresh)
+                else:
+                    slabs[i] = kept - factor * scaled
                 for m in range(k + 1, width):
                     cols[m][i] = cols[m][i] - factor * later[m - k - 1]
-        for k in range(width):
-            slabs[g] = jnp.where(row == at + k, rows[k], slabs[g])
     return slabs
 
 
@@ -348,12 +384,13 @@
         new_search[:, s, :] = result[:, wide + LANES * s : wide + LANES * (s + 1)]
 
 
-def call(kernel, outs, *args, scratch=(), place=VMEM):
+def call(kernel, outs, *args, scratch=(), place=VMEM, cost=None):
     shapes = [jax.ShapeDtypeStruct(shape, jnp.float32) for shape in outs]
     return pl.pallas_call(
         kernel,
         out_shape=shapes,
         in_specs=[place] * len(args),
+        cost_estimate=cost,
         out_specs=[VMEM] * len(shapes),
         scratch_shapes=[
             pltpu.VMEM(shape, jnp.float32) if isinstance(shape, tuple) else shape for shape in scratch
@@ -392,6 +429,15 @@
         *(pltpu.with_memory_space_constraint(x, pltpu.HBM) for x in (basis, search, conductivity)),
         scratch=blocks + [pltpu.SemaphoreType.DMA((3,))],
         place=pl.BlockSpec(memory_space=pltpu.HBM),
+    )
+    inner_x, inner_p = call(
+        inner,
+        [(cells_x, modes, flat)] * 2,
+        basis,
+        search,
+        conductivity,
+        scratch=[(4, ROWS, LANES)],
+        cost=pl.CostEstimate(flops=4 << 20, bytes_accessed=1 << 20, transcendentals=0),
     )
     row_two = paired(rows[1], "gx", 1)
     row_one = paired(rows[0], "gx", 0)
@@ -413,6 +459,8 @@
         basis,
         search,
         conductivity,
+        inner_x,
+        inner_p,
         lo,
         hi,
         side_two,

time: 77.6 us -> 75.9 us (0.978)
  Pallas kernels: 11.7 us -> 10.5 us
    pallas_call x4 -> x5, Pallas kernels: 11.7 us -> 10.5 us  [call(): pl.pallas_call(kernel, out_shape=shapes, in_specs=[place] * len(args), co...]
  transfers between devices with their start and end apart: 4 -> 4, of which waited for: 2 -> 2; matrix products, arithmetic and copies ran while one was open for 0% -> 0% of each run, Pallas kernels for 0% -> 1%
where the time goes in v4:
time: 75.9 us; the launch traced here: 75.6 us
  blocking collectives  47.7 us (63%)
  starting transfers between devices  14.6 us (19%)
  Pallas kernels  10.5 us (14%)
  waiting for transfers between devices  1.85 us (2%)
    all_to_all x3, blocking collectives, exchanged(): return lax.all_to_all(array, axis, 0, 0, tiled=True)  47.7 us
    ppermute x4, starting transfers between devices, paired(): return lax.ppermute(array, axis, pairs + [(j, i) for i, j in pairs])  14.6 us
    pallas_call x5, Pallas kernels, call(): pl.pallas_call(kernel, out_shape=shapes, in_specs=[place] * len(args), co...  10.5 us
    ppermute x4, waiting for transfers between devices, paired(): return lax.ppermute(array, axis, pairs + [(j, i) for i, j in pairs])  1.85 us
  transfers between devices with their start and end apart: 4, of which 2 were waited for; matrix products, arithmetic and copies ran while one was open for 0% of the time, Pallas kernels for 1%

profile of v4, /device:TPU:1, one launch (start us, length us, event | category | flops | bytes accessed | tf_op | source)
XLA Modules:
  0.0 75.6 jit_solution(14190938485312286090)
XLA Ops:
  0.6 0.0 copy-start.1
  0.6 0.0 copy-start
  0.7 0.0 copy-start.2
  0.7 1.1 %shard_map.68 = (f32[104,128]{1,0:T(8,128)S(1)}, f32[104,128]{1,0:T(8,128)S(1)}) custom-call(f32[32,8,128]{2,1,0:T(8,128)} %basis.5, f32[32,8,128]{2,1,0:T(8,128)} %search.5, f32[8,128]{1,0:T(8,128)} %cond.5), custom_call_target="tpu_custom_call" | custom-call | tf_op jit(solution)/shard_map/pallas_call | solution.py:389
  1.8 0.7 collective-permute-start
  2.5 6.4 %collective-permute-start.1 = (f32[104,128]{1,0:T(8,128)S(1)}, f32[104,128]{1,0:T(8,128)S(1)}, u32[]{:S(2)}, u32[]{:S(2)}) collective-permute-start(f32[104,128]{1,0:T(8,128)S(1)} %get-tuple-element.19), channel_id=1, source_target_pairs={{0,16},{32,48},{64,80},{96,112},{128,144},{160,176},{192,208},{224... | collective-permute-start | bytes 159752 | tf_op jit(solution)/shard_map/ppermute | solution.py:404
  8.9 0.0 collective-permute-done.row_two
  8.9 1.5 %collective-permute-done.1.row_one = f32[104,128]{1,0:T(8,128)S(1)} collective-permute-done((f32[104,128]{1,0:T(8,128)S(1)}, f32[104,128]{1,0:T(8,128)S(1)}, u32[]{:S(2)}, u32[]{:S(2)}) %collective-permute-start.1) | collective-permute-done | bytes 53280 | tf_op jit(solution)/shard_map/ppermute | solution.py:404
  10.4 0.0 copy-done.1
  10.4 0.0 copy-done
  10.4 0.0 copy-done.2
  10.4 0.4 shard_map.69
  10.8 4.9 %collective-permute-start.2 = (f32[112,128]{1,0:T(8,128)S(1)}, f32[112,128]{1,0:T(8,128)S(1)}, u32[]{:S(2)}, u32[]{:S(2)}) collective-permute-start(f32[112,128]{1,0:T(8,128)S(1)} %get-tuple-element.22), channel_id=1, source_target_pairs={{1,2},{3,4},{5,6},{7,8},{9,10},{11,12},{13,14},{2,1},{4,3},{6,5},{... | collective-permute-start | bytes 172040 | tf_op jit(solution)/shard_map/ppermute | solution.py:404
  15.7 2.6 %collective-permute-start.3 = (f32[112,128]{1,0:T(8,128)S(1)}, f32[112,128]{1,0:T(8,128)S(1)}, u32[]{:S(2)}, u32[]{:S(2)}) collective-permute-start(f32[112,128]{1,0:T(8,128)S(1)} %get-tuple-element.23), channel_id=1, source_target_pairs={{0,1},{2,3},{4,5},{6,7},{8,9},{10,11},{12,13},{14,15},{1,0},{3,2},... | collective-permute-start | bytes 172040 | tf_op jit(solution)/shard_map/ppermute | solution.py:404
  18.3 0.5 shard_map.67
  18.8 0.0 collective-permute-done.2.side_two
  18.9 0.3 collective-permute-done.3.side_one
  19.2 1.8 %shard_map.70 = (f32[96,1024]{1,0:T(8,128)S(1)}, f32[64,128]{1,0:T(8,128)S(1)}) custom-call(f32[32,8,128]{2,1,0:T(8,128)S(1)} %copy-done, f32[32,8,128]{2,1,0:T(8,128)S(1)} %copy-done.1, f32[8,128]{1,0:T(8,128)S(1)} %copy-done.2, f32[8,32,128]{2,1,0:T(8,128)S(1)} %get-tuple-element.16.inner_x, f32[8,32,128]{2,1,0:T(8,128)S(1)} %get-tuple-element.17.inner_p, ...), custom_call_target="tpu_custom_call" | custom-call | tf_op jit(solution)/shard_map/pallas_call | solution.py:389
  21.0 14.4 %all_to_all.23 = f32[16,4,128]{2,1,0:T(4,128)S(1)} all-to-all(f32[16,4,128]{2,1,0:T(4,128)S(1)} %bitcast.5), channel_id=1, replica_groups=mesh['gx'=32,'gy'=16] {'gy'}, dimensions={0} | all-to-all | bytes 65536 | tf_op jit(solution)/shard_map/all_to_all | solution.py:408
  35.4 21.6 %all_to_all.24 = f32[32,4,128]{2,1,0:T(4,128)S(1)} all-to-all(f32[32,4,128]{2,1,0:T(4,128)S(1)} %tile.4), channel_id=1, replica_groups=mesh['gx'=32,'gy'=16] {'gx'}, dimensions={0} | all-to-all | bytes 131072 | tf_op jit(solution)/shard_map/all_to_all | solution.py:408
  57.1 0.0 copy-start.3
  57.2 11.7 %all_to_all.25 = f32[16,4,128]{2,1,0:T(4,128)S(1)} all-to-all(f32[16,4,128]{2,1,0:T(4,128)S(1)} %tile.5), channel_id=1, replica_groups=mesh['gx'=32,'gy'=16] {'gy'}, dimensions={0} | all-to-all | bytes 65536 | tf_op jit(solution)/shard_map/all_to_all | solution.py:408
  68.9 0.0 copy-done.3
  68.9 6.7 %shard_map.71 = (f32[32,8,128]{2,1,0:T(8,128)}, f32[32,8,128]{2,1,0:T(8,128)}, f32[1,32]{1,0:T(1,128)}) custom-call(f32[64,128]{1,0:T(8,128)S(1)} %bitcast.4, s32[32,96]{1,0:T(8,128)S(1)} %bitcast.6, f32[96,1024]{1,0:T(8,128)S(1)} %get-tuple-element.25.refs_2_), custom_call_target="tpu_custom_call" | custom-call | tf_op jit(solution)/shard_map/pallas_call | solution.py:389
  (4 shorter events, 0.1 us)
Async XLA Ops:
  0.6 9.8 %copy-start.1 = (f32[32,8,128]{2,1,0:T(8,128)S(1)}, f32[32,8,128]{2,1,0:T(8,128)}, u32[]{:S(2)}) copy-start(f32[32,8,128]{2,1,0:T(8,128)} %search.5) | copy-start | bytes 393220
  0.6 9.8 %copy-start = (f32[32,8,128]{2,1,0:T(8,128)S(1)}, f32[32,8,128]{2,1,0:T(8,128)}, u32[]{:S(2)}) copy-start(f32[32,8,128]{2,1,0:T(8,128)} %basis.5) | copy-start | bytes 393220
  0.7 9.7 %copy-start.2 = (f32[8,128]{1,0:T(8,128)S(1)}, f32[8,128]{1,0:T(8,128)}, u32[]{:S(2)}) copy-start(f32[8,128]{1,0:T(8,128)} %cond.5) | copy-start | bytes 12292
  1.8 7.1 %collective-permute-start = (f32[104,128]{1,0:T(8,128)S(1)}, f32[104,128]{1,0:T(8,128)S(1)}, u32[]{:S(2)}, u32[]{:S(2)}) collective-permute-start(f32[104,128]{1,0:T(8,128)S(1)} %get-tuple-element.18), channel_id=1, source_target_pairs={{16,32},{48,64},{80,96},{112,128},{144,160},{176,192},{208,224},{2... | collective-permute-start | bytes 159752 | tf_op jit(solution)/shard_map/ppermute | solution.py:404
  2.5 7.9 %collective-permute-start.1 = (f32[104,128]{1,0:T(8,128)S(1)}, f32[104,128]{1,0:T(8,128)S(1)}, u32[]{:S(2)}, u32[]{:S(2)}) collective-permute-start(f32[104,128]{1,0:T(8,128)S(1)} %get-tuple-element.19), channel_id=1, source_target_pairs={{0,16},{32,48},{64,80},{96,112},{128,144},{160,176},{192,208},{224... | collective-permute-start | bytes 159752 | tf_op jit(solution)/shard_map/ppermute | solution.py:404
  10.8 8.1 %collective-permute-start.2 = (f32[112,128]{1,0:T(8,128)S(1)}, f32[112,128]{1,0:T(8,128)S(1)}, u32[]{:S(2)}, u32[]{:S(2)}) collective-permute-start(f32[112,128]{1,0:T(8,128)S(1)} %get-tuple-element.22), channel_id=1, source_target_pairs={{1,2},{3,4},{5,6},{7,8},{9,10},{11,12},{13,14},{2,1},{4,3},{6,5},{... | collective-permute-start | bytes 172040 | tf_op jit(solution)/shard_map/ppermute | solution.py:404
  15.7 3.5 %collective-permute-start.3 = (f32[112,128]{1,0:T(8,128)S(1)}, f32[112,128]{1,0:T(8,128)S(1)}, u32[]{:S(2)}, u32[]{:S(2)}) collective-permute-start(f32[112,128]{1,0:T(8,128)S(1)} %get-tuple-element.23), channel_id=1, source_target_pairs={{0,1},{2,3},{4,5},{6,7},{8,9},{10,11},{12,13},{14,15},{1,0},{3,2},... | collective-permute-start | bytes 172040 | tf_op jit(solution)/shard_map/ppermute | solution.py:404
  57.1 11.7 %copy-start.3 = (s32[96,32]{0,1:T(8,128)S(1)}, s32[96,32]{0,1:T(8,128)}, u32[]{:S(2)}) copy-start(s32[96,32]{0,1:T(8,128)} %param.7) | copy-start | bytes 36868

commit v5 on v4

--- a/solution.py
+++ b/solution.py
@@ -293,37 +293,37 @@
 def eliminate(slabs):
     slabs = list(slabs)
     count = len(slabs)
-    lane = lanes((8, LANES))
-    row = lax.broadcasted_iota(jnp.int32, (8, LANES), 0)
-    width = 4
-    for start in range(0, 8 * count, width):
-        g = start // 8
-        cols = [
-            {i: jnp.broadcast_to(slabs[i][:, start + k : start + k + 1], (8, LANES)) for i in range(g, count)}
-            for k in range(width)
-        ]
-        for k in range(width):
-            j = start + k
-            at = j % 8
-            pivot = cols[k][g][at : at + 1, :]
-            root = lax.rsqrt(pivot)
+    tile = (8, LANES)
+    lane = lanes(tile)
+    row = lax.broadcasted_iota(jnp.int32, tile, 0)
+
+    def spread(slab, column):
+        return jnp.broadcast_to(slabs[slab][:, column : column + 1], tile)
+
+    ahead = [spread(0, k) for k in range(8)]
+    for g in range(count):
+        cols = [[ahead[k]] + [spread(i, 8 * g + k) for i in range(g + 1, count)] for k in range(8)]
+        ahead = [spread(g + 1, 8 * g + 8 + k) for k in range(8)] if g + 1 < count else []
+        for k in range(8):
+            here = lane == 8 * g + k
+            root = lax.rsqrt(cols[k][0][k : k + 1, :])
             inverse = root * root
-            here = lane[:1] == j
-            pivot_row = jnp.where(here, 1.0, slabs[g][at : at + 1, :])
+            pivot_row = jnp.where(here[:1], 1.0, slabs[g][k : k + 1, :])
             scaled = pivot_row * inverse
-            later = [cols[m][g][at : at + 1, :] * inverse for m in range(k + 1, width)]
-            for i in range(g, count):
+            later = [cols[m][0][k : k + 1, :] * inverse for m in range(k + 1, 8)]
+            for i in range(count - g):
                 factor = cols[k][i]
-                kept = jnp.where(lane == j, 0.0, slabs[i])
-                if i == g:
-                    factor = jnp.where(row > at, factor, 0.0)
-                    kept = jnp.where(row > at, kept, slabs[i])
-                    fresh = kept - factor * scaled
-                    slabs[i] = jnp.where(row == at, pivot_row * root, fresh)
+                if i == 0:
+                    factor = jnp.where(row > k, factor, 0.0)
+                    kept = jnp.where(here & (row > k), 0.0, slabs[g])
+                    slabs[g] = jnp.where(row == k, pivot_row * root, kept - factor * scaled)
                 else:
-                    slabs[i] = kept - factor * scaled
-                for m in range(k + 1, width):
+                    slabs[g + i] = jnp.where(here, 0.0, slabs[g + i]) - factor * scaled
+                for m in range(k + 1, 8):
                     cols[m][i] = cols[m][i] - factor * later[m - k - 1]
+            if ahead:
+                below = cols[k][1]
+                ahead = [ahead[c] - below * (below[c : c + 1, :] * inverse) for c in range(8)]
     return slabs
 
 

time: 75.9 us -> 74.3 us (0.979)
  Pallas kernels: 10.5 us -> 8.93 us
    pallas_call x5, Pallas kernels: 10.5 us -> 8.93 us  [call(): pl.pallas_call(kernel, out_shape=shapes, in_specs=[place] * len(args), co...]
where the time goes in v5:
time: 74.3 us; the launch traced here: 74 us
  blocking collectives  47.7 us (64%)
  starting transfers between devices  14.6 us (20%)
  Pallas kernels  8.93 us (12%)
  waiting for transfers between devices  1.85 us (2%)
    all_to_all x3, blocking collectives, exchanged(): return lax.all_to_all(array, axis, 0, 0, tiled=True)  47.7 us
    ppermute x4, starting transfers between devices, paired(): return lax.ppermute(array, axis, pairs + [(j, i) for i, j in pairs])  14.6 us
    pallas_call x5, Pallas kernels, call(): pl.pallas_call(kernel, out_shape=shapes, in_specs=[place] * len(args), co...  8.93 us
    ppermute x4, waiting for transfers between devices, paired(): return lax.ppermute(array, axis, pairs + [(j, i) for i, j in pairs])  1.85 us
  transfers between devices with their start and end apart: 4, of which 2 were waited for; matrix products, arithmetic and copies ran while one was open for 0% of the time, Pallas kernels for 1%

profile of v5, /device:TPU:1, one launch (start us, length us, event | category | flops | bytes accessed | tf_op | source)
XLA Modules:
  0.0 74.0 jit_solution(3886665954728699849)
XLA Ops:
  0.6 0.0 copy-start.1
  0.6 0.0 copy-start
  0.7 0.0 copy-start.2
  0.7 1.1 %shard_map.68 = (f32[104,128]{1,0:T(8,128)S(1)}, f32[104,128]{1,0:T(8,128)S(1)}) custom-call(f32[32,8,128]{2,1,0:T(8,128)} %basis.5, f32[32,8,128]{2,1,0:T(8,128)} %search.5, f32[8,128]{1,0:T(8,128)} %cond.5), custom_call_target="tpu_custom_call" | custom-call | tf_op jit(solution)/shard_map/pallas_call | solution.py:389
  1.8 0.7 collective-permute-start
  2.5 6.4 %collective-permute-start.1 = (f32[104,128]{1,0:T(8,128)S(1)}, f32[104,128]{1,0:T(8,128)S(1)}, u32[]{:S(2)}, u32[]{:S(2)}) collective-permute-start(f32[104,128]{1,0:T(8,128)S(1)} %get-tuple-element.19), channel_id=1, source_target_pairs={{0,16},{32,48},{64,80},{96,112},{128,144},{160,176},{192,208},{224... | collective-permute-start | bytes 159752 | tf_op jit(solution)/shard_map/ppermute | solution.py:404
  8.9 0.0 collective-permute-done.row_two
  8.9 1.5 %collective-permute-done.1.row_one = f32[104,128]{1,0:T(8,128)S(1)} collective-permute-done((f32[104,128]{1,0:T(8,128)S(1)}, f32[104,128]{1,0:T(8,128)S(1)}, u32[]{:S(2)}, u32[]{:S(2)}) %collective-permute-start.1) | collective-permute-done | bytes 53280 | tf_op jit(solution)/shard_map/ppermute | solution.py:404
  10.4 0.0 copy-done.1
  10.4 0.0 copy-done
  10.4 0.0 copy-done.2
  10.4 0.4 shard_map.69
  10.8 4.9 %collective-permute-start.2 = (f32[112,128]{1,0:T(8,128)S(1)}, f32[112,128]{1,0:T(8,128)S(1)}, u32[]{:S(2)}, u32[]{:S(2)}) collective-permute-start(f32[112,128]{1,0:T(8,128)S(1)} %get-tuple-element.22), channel_id=1, source_target_pairs={{1,2},{3,4},{5,6},{7,8},{9,10},{11,12},{13,14},{2,1},{4,3},{6,5},{... | collective-permute-start | bytes 172040 | tf_op jit(solution)/shard_map/ppermute | solution.py:404
  15.7 2.6 %collective-permute-start.3 = (f32[112,128]{1,0:T(8,128)S(1)}, f32[112,128]{1,0:T(8,128)S(1)}, u32[]{:S(2)}, u32[]{:S(2)}) collective-permute-start(f32[112,128]{1,0:T(8,128)S(1)} %get-tuple-element.23), channel_id=1, source_target_pairs={{0,1},{2,3},{4,5},{6,7},{8,9},{10,11},{12,13},{14,15},{1,0},{3,2},... | collective-permute-start | bytes 172040 | tf_op jit(solution)/shard_map/ppermute | solution.py:404
  18.3 0.5 shard_map.67
  18.8 0.0 collective-permute-done.2.side_two
  18.9 0.3 collective-permute-done.3.side_one
  19.2 1.8 %shard_map.70 = (f32[96,1024]{1,0:T(8,128)S(1)}, f32[64,128]{1,0:T(8,128)S(1)}) custom-call(f32[32,8,128]{2,1,0:T(8,128)S(1)} %copy-done, f32[32,8,128]{2,1,0:T(8,128)S(1)} %copy-done.1, f32[8,128]{1,0:T(8,128)S(1)} %copy-done.2, f32[8,32,128]{2,1,0:T(8,128)S(1)} %get-tuple-element.16.inner_x, f32[8,32,128]{2,1,0:T(8,128)S(1)} %get-tuple-element.17.inner_p, ...), custom_call_target="tpu_custom_call" | custom-call | tf_op jit(solution)/shard_map/pallas_call | solution.py:389
  21.0 14.4 %all_to_all.23 = f32[16,4,128]{2,1,0:T(4,128)S(1)} all-to-all(f32[16,4,128]{2,1,0:T(4,128)S(1)} %bitcast.5), channel_id=1, replica_groups=mesh['gx'=32,'gy'=16] {'gy'}, dimensions={0} | all-to-all | bytes 65536 | tf_op jit(solution)/shard_map/all_to_all | solution.py:408
  35.4 21.6 %all_to_all.24 = f32[32,4,128]{2,1,0:T(4,128)S(1)} all-to-all(f32[32,4,128]{2,1,0:T(4,128)S(1)} %tile.4), channel_id=1, replica_groups=mesh['gx'=32,'gy'=16] {'gx'}, dimensions={0} | all-to-all | bytes 131072 | tf_op jit(solution)/shard_map/all_to_all | solution.py:408
  57.1 0.0 copy-start.3
  57.2 11.7 %all_to_all.25 = f32[16,4,128]{2,1,0:T(4,128)S(1)} all-to-all(f32[16,4,128]{2,1,0:T(4,128)S(1)} %tile.5), channel_id=1, replica_groups=mesh['gx'=32,'gy'=16] {'gy'}, dimensions={0} | all-to-all | bytes 65536 | tf_op jit(solution)/shard_map/all_to_all | solution.py:408
  68.9 0.0 copy-done.3
  68.9 5.1 %shard_map.71 = (f32[32,8,128]{2,1,0:T(8,128)}, f32[32,8,128]{2,1,0:T(8,128)}, f32[1,32]{1,0:T(1,128)}) custom-call(f32[64,128]{1,0:T(8,128)S(1)} %bitcast.4, s32[32,96]{1,0:T(8,128)S(1)} %bitcast.6, f32[96,1024]{1,0:T(8,128)S(1)} %get-tuple-element.25.refs_2_), custom_call_target="tpu_custom_call" | custom-call | tf_op jit(solution)/shard_map/pallas_call | solution.py:389
  (4 shorter events, 0.1 us)
Async XLA Ops:
  0.6 9.8 %copy-start.1 = (f32[32,8,128]{2,1,0:T(8,128)S(1)}, f32[32,8,128]{2,1,0:T(8,128)}, u32[]{:S(2)}) copy-start(f32[32,8,128]{2,1,0:T(8,128)} %search.5) | copy-start | bytes 393220
  0.6 9.8 %copy-start = (f32[32,8,128]{2,1,0:T(8,128)S(1)}, f32[32,8,128]{2,1,0:T(8,128)}, u32[]{:S(2)}) copy-start(f32[32,8,128]{2,1,0:T(8,128)} %basis.5) | copy-start | bytes 393220
  0.7 9.7 %copy-start.2 = (f32[8,128]{1,0:T(8,128)S(1)}, f32[8,128]{1,0:T(8,128)}, u32[]{:S(2)}) copy-start(f32[8,128]{1,0:T(8,128)} %cond.5) | copy-start | bytes 12292
  1.8 7.1 %collective-permute-start = (f32[104,128]{1,0:T(8,128)S(1)}, f32[104,128]{1,0:T(8,128)S(1)}, u32[]{:S(2)}, u32[]{:S(2)}) collective-permute-start(f32[104,128]{1,0:T(8,128)S(1)} %get-tuple-element.18), channel_id=1, source_target_pairs={{16,32},{48,64},{80,96},{112,128},{144,160},{176,192},{208,224},{2... | collective-permute-start | bytes 159752 | tf_op jit(solution)/shard_map/ppermute | solution.py:404
  2.5 7.9 %collective-permute-start.1 = (f32[104,128]{1,0:T(8,128)S(1)}, f32[104,128]{1,0:T(8,128)S(1)}, u32[]{:S(2)}, u32[]{:S(2)}) collective-permute-start(f32[104,128]{1,0:T(8,128)S(1)} %get-tuple-element.19), channel_id=1, source_target_pairs={{0,16},{32,48},{64,80},{96,112},{128,144},{160,176},{192,208},{224... | collective-permute-start | bytes 159752 | tf_op jit(solution)/shard_map/ppermute | solution.py:404
  10.8 8.1 %collective-permute-start.2 = (f32[112,128]{1,0:T(8,128)S(1)}, f32[112,128]{1,0:T(8,128)S(1)}, u32[]{:S(2)}, u32[]{:S(2)}) collective-permute-start(f32[112,128]{1,0:T(8,128)S(1)} %get-tuple-element.22), channel_id=1, source_target_pairs={{1,2},{3,4},{5,6},{7,8},{9,10},{11,12},{13,14},{2,1},{4,3},{6,5},{... | collective-permute-start | bytes 172040 | tf_op jit(solution)/shard_map/ppermute | solution.py:404
  15.7 3.5 %collective-permute-start.3 = (f32[112,128]{1,0:T(8,128)S(1)}, f32[112,128]{1,0:T(8,128)S(1)}, u32[]{:S(2)}, u32[]{:S(2)}) collective-permute-start(f32[112,128]{1,0:T(8,128)S(1)} %get-tuple-element.23), channel_id=1, source_target_pairs={{0,1},{2,3},{4,5},{6,7},{8,9},{10,11},{12,13},{14,15},{1,0},{3,2},... | collective-permute-start | bytes 172040 | tf_op jit(solution)/shard_map/ppermute | solution.py:404
  57.1 11.7 %copy-start.3 = (s32[96,32]{0,1:T(8,128)S(1)}, s32[96,32]{0,1:T(8,128)}, u32[]{:S(2)}) copy-start(s32[96,32]{0,1:T(8,128)} %param.7) | copy-start | bytes 36868

commit v6 on v5

--- a/solution.py
+++ b/solution.py
@@ -306,11 +306,12 @@
         ahead = [spread(g + 1, 8 * g + 8 + k) for k in range(8)] if g + 1 < count else []
         for k in range(8):
             here = lane == 8 * g + k
-            root = lax.rsqrt(cols[k][0][k : k + 1, :])
+            root = lax.rsqrt(jnp.broadcast_to(cols[k][0][k : k + 1, :], tile))
             inverse = root * root
-            pivot_row = jnp.where(here[:1], 1.0, slabs[g][k : k + 1, :])
+            pivot_row = jnp.where(here, 1.0, jnp.broadcast_to(slabs[g][k : k + 1, :], tile))
             scaled = pivot_row * inverse
-            later = [cols[m][0][k : k + 1, :] * inverse for m in range(k + 1, 8)]
+            entries = [jnp.broadcast_to(cols[m][0][k : k + 1, :], tile) for m in range(k + 1, 8)]
+            later = [entry * inverse for entry in entries]
             for i in range(count - g):
                 factor = cols[k][i]
                 if i == 0:
@@ -320,10 +321,13 @@
                 else:
                     slabs[g + i] = jnp.where(here, 0.0, slabs[g + i]) - factor * scaled
                 for m in range(k + 1, 8):
-                    cols[m][i] = cols[m][i] - factor * later[m - k - 1]
+                    if i == 0:
+                        cols[m][i] = cols[m][i] - (factor * entries[m - k - 1]) * inverse
+                    else:
+                        cols[m][i] = cols[m][i] - factor * later[m - k - 1]
             if ahead:
                 below = cols[k][1]
-                ahead = [ahead[c] - below * (below[c : c + 1, :] * inverse) for c in range(8)]
+                ahead = [ahead[c] - (below * below[c : c + 1, :]) * inverse for c in range(8)]
     return slabs
 
 

time: 74.3 us -> 74.6 us (level)
  no operation moved by 1% of the time
where the time goes in v6:
time: 74.6 us; the launch traced here: 74.3 us
  blocking collectives  47.7 us (64%)
  starting transfers between devices  14.6 us (20%)
  Pallas kernels  9.24 us (12%)
  waiting for transfers between devices  1.85 us (2%)
    all_to_all x3, blocking collectives, exchanged(): return lax.all_to_all(array, axis, 0, 0, tiled=True)  47.7 us
    ppermute x4, starting transfers between devices, paired(): return lax.ppermute(array, axis, pairs + [(j, i) for i, j in pairs])  14.6 us
    pallas_call x5, Pallas kernels, call(): pl.pallas_call(kernel, out_shape=shapes, in_specs=[place] * len(args), co...  9.24 us
    ppermute x4, waiting for transfers between devices, paired(): return lax.ppermute(array, axis, pairs + [(j, i) for i, j in pairs])  1.85 us
  transfers between devices with their start and end apart: 4, of which 2 were waited for; matrix products, arithmetic and copies ran while one was open for 0% of the time, Pallas kernels for 1%

profile of v6, /device:TPU:1, one launch (start us, length us, event | category | flops | bytes accessed | tf_op | source)
XLA Modules:
  0.0 74.3 jit_solution(1010281861840608691)
XLA Ops:
  0.6 0.0 copy-start.1
  0.6 0.0 copy-start
  0.7 0.0 copy-start.2
  0.7 1.1 %shard_map.68 = (f32[104,128]{1,0:T(8,128)S(1)}, f32[104,128]{1,0:T(8,128)S(1)}) custom-call(f32[32,8,128]{2,1,0:T(8,128)} %basis.5, f32[32,8,128]{2,1,0:T(8,128)} %search.5, f32[8,128]{1,0:T(8,128)} %cond.5), custom_call_target="tpu_custom_call" | custom-call | tf_op jit(solution)/shard_map/pallas_call | solution.py:393
  1.8 0.7 collective-permute-start
  2.5 6.4 %collective-permute-start.1 = (f32[104,128]{1,0:T(8,128)S(1)}, f32[104,128]{1,0:T(8,128)S(1)}, u32[]{:S(2)}, u32[]{:S(2)}) collective-permute-start(f32[104,128]{1,0:T(8,128)S(1)} %get-tuple-element.19), channel_id=1, source_target_pairs={{0,16},{32,48},{64,80},{96,112},{128,144},{160,176},{192,208},{224... | collective-permute-start | bytes 159752 | tf_op jit(solution)/shard_map/ppermute | solution.py:408
  8.9 0.0 collective-permute-done.row_two
  8.9 1.5 %collective-permute-done.1.row_one = f32[104,128]{1,0:T(8,128)S(1)} collective-permute-done((f32[104,128]{1,0:T(8,128)S(1)}, f32[104,128]{1,0:T(8,128)S(1)}, u32[]{:S(2)}, u32[]{:S(2)}) %collective-permute-start.1) | collective-permute-done | bytes 53280 | tf_op jit(solution)/shard_map/ppermute | solution.py:408
  10.4 0.0 copy-done.1
  10.4 0.0 copy-done
  10.4 0.0 copy-done.2
  10.4 0.4 shard_map.69
  10.8 4.9 %collective-permute-start.2 = (f32[112,128]{1,0:T(8,128)S(1)}, f32[112,128]{1,0:T(8,128)S(1)}, u32[]{:S(2)}, u32[]{:S(2)}) collective-permute-start(f32[112,128]{1,0:T(8,128)S(1)} %get-tuple-element.22), channel_id=1, source_target_pairs={{1,2},{3,4},{5,6},{7,8},{9,10},{11,12},{13,14},{2,1},{4,3},{6,5},{... | collective-permute-start | bytes 172040 | tf_op jit(solution)/shard_map/ppermute | solution.py:408
  15.7 2.6 %collective-permute-start.3 = (f32[112,128]{1,0:T(8,128)S(1)}, f32[112,128]{1,0:T(8,128)S(1)}, u32[]{:S(2)}, u32[]{:S(2)}) collective-permute-start(f32[112,128]{1,0:T(8,128)S(1)} %get-tuple-element.23), channel_id=1, source_target_pairs={{0,1},{2,3},{4,5},{6,7},{8,9},{10,11},{12,13},{14,15},{1,0},{3,2},... | collective-permute-start | bytes 172040 | tf_op jit(solution)/shard_map/ppermute | solution.py:408
  18.3 0.5 shard_map.67
  18.8 0.0 collective-permute-done.2.side_two
  18.9 0.3 collective-permute-done.3.side_one
  19.2 1.8 %shard_map.70 = (f32[96,1024]{1,0:T(8,128)S(1)}, f32[64,128]{1,0:T(8,128)S(1)}) custom-call(f32[32,8,128]{2,1,0:T(8,128)S(1)} %copy-done, f32[32,8,128]{2,1,0:T(8,128)S(1)} %copy-done.1, f32[8,128]{1,0:T(8,128)S(1)} %copy-done.2, f32[8,32,128]{2,1,0:T(8,128)S(1)} %get-tuple-element.16.inner_x, f32[8,32,128]{2,1,0:T(8,128)S(1)} %get-tuple-element.17.inner_p, ...), custom_call_target="tpu_custom_call" | custom-call | tf_op jit(solution)/shard_map/pallas_call | solution.py:393
  21.0 14.4 %all_to_all.23 = f32[16,4,128]{2,1,0:T(4,128)S(1)} all-to-all(f32[16,4,128]{2,1,0:T(4,128)S(1)} %bitcast.5), channel_id=1, replica_groups=mesh['gx'=32,'gy'=16] {'gy'}, dimensions={0} | all-to-all | bytes 65536 | tf_op jit(solution)/shard_map/all_to_all | solution.py:412
  35.4 21.6 %all_to_all.24 = f32[32,4,128]{2,1,0:T(4,128)S(1)} all-to-all(f32[32,4,128]{2,1,0:T(4,128)S(1)} %tile.4), channel_id=1, replica_groups=mesh['gx'=32,'gy'=16] {'gx'}, dimensions={0} | all-to-all | bytes 131072 | tf_op jit(solution)/shard_map/all_to_all | solution.py:412
  57.1 0.0 copy-start.3
  57.2 11.7 %all_to_all.25 = f32[16,4,128]{2,1,0:T(4,128)S(1)} all-to-all(f32[16,4,128]{2,1,0:T(4,128)S(1)} %tile.5), channel_id=1, replica_groups=mesh['gx'=32,'gy'=16] {'gy'}, dimensions={0} | all-to-all | bytes 65536 | tf_op jit(solution)/shard_map/all_to_all | solution.py:412
  68.9 0.0 copy-done.3
  68.9 5.4 %shard_map.71 = (f32[32,8,128]{2,1,0:T(8,128)}, f32[32,8,128]{2,1,0:T(8,128)}, f32[1,32]{1,0:T(1,128)}) custom-call(f32[64,128]{1,0:T(8,128)S(1)} %bitcast.4, s32[32,96]{1,0:T(8,128)S(1)} %bitcast.6, f32[96,1024]{1,0:T(8,128)S(1)} %get-tuple-element.25.refs_2_), custom_call_target="tpu_custom_call" | custom-call | tf_op jit(solution)/shard_map/pallas_call | solution.py:393
  (4 shorter events, 0.1 us)
Async XLA Ops:
  0.6 9.8 %copy-start.1 = (f32[32,8,128]{2,1,0:T(8,128)S(1)}, f32[32,8,128]{2,1,0:T(8,128)}, u32[]{:S(2)}) copy-start(f32[32,8,128]{2,1,0:T(8,128)} %search.5) | copy-start | bytes 393220
  0.6 9.8 %copy-start = (f32[32,8,128]{2,1,0:T(8,128)S(1)}, f32[32,8,128]{2,1,0:T(8,128)}, u32[]{:S(2)}) copy-start(f32[32,8,128]{2,1,0:T(8,128)} %basis.5) | copy-start | bytes 393220
  0.7 9.7 %copy-start.2 = (f32[8,128]{1,0:T(8,128)S(1)}, f32[8,128]{1,0:T(8,128)}, u32[]{:S(2)}) copy-start(f32[8,128]{1,0:T(8,128)} %cond.5) | copy-start | bytes 12292
  1.8 7.1 %collective-permute-start = (f32[104,128]{1,0:T(8,128)S(1)}, f32[104,128]{1,0:T(8,128)S(1)}, u32[]{:S(2)}, u32[]{:S(2)}) collective-permute-start(f32[104,128]{1,0:T(8,128)S(1)} %get-tuple-element.18), channel_id=1, source_target_pairs={{16,32},{48,64},{80,96},{112,128},{144,160},{176,192},{208,224},{2... | collective-permute-start | bytes 159752 | tf_op jit(solution)/shard_map/ppermute | solution.py:408
  2.5 7.9 %collective-permute-start.1 = (f32[104,128]{1,0:T(8,128)S(1)}, f32[104,128]{1,0:T(8,128)S(1)}, u32[]{:S(2)}, u32[]{:S(2)}) collective-permute-start(f32[104,128]{1,0:T(8,128)S(1)} %get-tuple-element.19), channel_id=1, source_target_pairs={{0,16},{32,48},{64,80},{96,112},{128,144},{160,176},{192,208},{224... | collective-permute-start | bytes 159752 | tf_op jit(solution)/shard_map/ppermute | solution.py:408
  10.8 8.1 %collective-permute-start.2 = (f32[112,128]{1,0:T(8,128)S(1)}, f32[112,128]{1,0:T(8,128)S(1)}, u32[]{:S(2)}, u32[]{:S(2)}) collective-permute-start(f32[112,128]{1,0:T(8,128)S(1)} %get-tuple-element.22), channel_id=1, source_target_pairs={{1,2},{3,4},{5,6},{7,8},{9,10},{11,12},{13,14},{2,1},{4,3},{6,5},{... | collective-permute-start | bytes 172040 | tf_op jit(solution)/shard_map/ppermute | solution.py:408
  15.7 3.5 %collective-permute-start.3 = (f32[112,128]{1,0:T(8,128)S(1)}, f32[112,128]{1,0:T(8,128)S(1)}, u32[]{:S(2)}, u32[]{:S(2)}) collective-permute-start(f32[112,128]{1,0:T(8,128)S(1)} %get-tuple-element.23), channel_id=1, source_target_pairs={{0,1},{2,3},{4,5},{6,7},{8,9},{10,11},{12,13},{14,15},{1,0},{3,2},... | collective-permute-start | bytes 172040 | tf_op jit(solution)/shard_map/ppermute | solution.py:408
  57.1 11.7 %copy-start.3 = (s32[96,32]{0,1:T(8,128)S(1)}, s32[96,32]{0,1:T(8,128)}, u32[]{:S(2)}) copy-start(s32[96,32]{0,1:T(8,128)} %param.7) | copy-start | bytes 36868

commit v7 on v5

--- a/solution.py
+++ b/solution.py
@@ -320,7 +320,10 @@
                 else:
                     slabs[g + i] = jnp.where(here, 0.0, slabs[g + i]) - factor * scaled
                 for m in range(k + 1, 8):
-                    cols[m][i] = cols[m][i] - factor * later[m - k - 1]
+                    if i == 0 and m == k + 1:
+                        cols[m][i] = cols[m][i] - (factor * cols[m][i][k : k + 1, :]) * inverse
+                    else:
+                        cols[m][i] = cols[m][i] - factor * later[m - k - 1]
             if ahead:
                 below = cols[k][1]
                 ahead = [ahead[c] - below * (below[c : c + 1, :] * inverse) for c in range(8)]

time: 74.3 us -> 74.2 us (level)
  no operation moved by 1% of the time
where the time goes in v7:
time: 74.2 us; the launch traced here: 73.8 us
  blocking collectives  47.7 us (64%)
  starting transfers between devices  14.6 us (20%)
  Pallas kernels  8.78 us (12%)
  waiting for transfers between devices  1.85 us (2%)
    all_to_all x3, blocking collectives, exchanged(): return lax.all_to_all(array, axis, 0, 0, tiled=True)  47.7 us
    ppermute x4, starting transfers between devices, paired(): return lax.ppermute(array, axis, pairs + [(j, i) for i, j in pairs])  14.6 us
    pallas_call x5, Pallas kernels, call(): pl.pallas_call(kernel, out_shape=shapes, in_specs=[place] * len(args), co...  8.78 us
    ppermute x4, waiting for transfers between devices, paired(): return lax.ppermute(array, axis, pairs + [(j, i) for i, j in pairs])  1.85 us
  transfers between devices with their start and end apart: 4, of which 2 were waited for; matrix products, arithmetic and copies ran while one was open for 0% of the time, Pallas kernels for 1%

profile of v7, /device:TPU:1, one launch (start us, length us, event | category | flops | bytes accessed | tf_op | source)
XLA Modules:
  0.0 73.8 jit_solution(7322712083729475792)
XLA Ops:
  0.6 0.0 copy-start.1
  0.6 0.0 copy-start
  0.7 0.0 copy-start.2
  0.7 1.1 %shard_map.68 = (f32[104,128]{1,0:T(8,128)S(1)}, f32[104,128]{1,0:T(8,128)S(1)}) custom-call(f32[32,8,128]{2,1,0:T(8,128)} %basis.5, f32[32,8,128]{2,1,0:T(8,128)} %search.5, f32[8,128]{1,0:T(8,128)} %cond.5), custom_call_target="tpu_custom_call" | custom-call | tf_op jit(solution)/shard_map/pallas_call | solution.py:392
  1.8 0.7 collective-permute-start
  2.5 6.4 %collective-permute-start.1 = (f32[104,128]{1,0:T(8,128)S(1)}, f32[104,128]{1,0:T(8,128)S(1)}, u32[]{:S(2)}, u32[]{:S(2)}) collective-permute-start(f32[104,128]{1,0:T(8,128)S(1)} %get-tuple-element.19), channel_id=1, source_target_pairs={{0,16},{32,48},{64,80},{96,112},{128,144},{160,176},{192,208},{224... | collective-permute-start | bytes 159752 | tf_op jit(solution)/shard_map/ppermute | solution.py:407
  8.9 0.0 collective-permute-done.row_two
  8.9 1.5 %collective-permute-done.1.row_one = f32[104,128]{1,0:T(8,128)S(1)} collective-permute-done((f32[104,128]{1,0:T(8,128)S(1)}, f32[104,128]{1,0:T(8,128)S(1)}, u32[]{:S(2)}, u32[]{:S(2)}) %collective-permute-start.1) | collective-permute-done | bytes 53280 | tf_op jit(solution)/shard_map/ppermute | solution.py:407
  10.4 0.0 copy-done.1
  10.4 0.0 copy-done
  10.4 0.0 copy-done.2
  10.4 0.4 shard_map.69
  10.8 4.9 %collective-permute-start.2 = (f32[112,128]{1,0:T(8,128)S(1)}, f32[112,128]{1,0:T(8,128)S(1)}, u32[]{:S(2)}, u32[]{:S(2)}) collective-permute-start(f32[112,128]{1,0:T(8,128)S(1)} %get-tuple-element.22), channel_id=1, source_target_pairs={{1,2},{3,4},{5,6},{7,8},{9,10},{11,12},{13,14},{2,1},{4,3},{6,5},{... | collective-permute-start | bytes 172040 | tf_op jit(solution)/shard_map/ppermute | solution.py:407
  15.7 2.6 %collective-permute-start.3 = (f32[112,128]{1,0:T(8,128)S(1)}, f32[112,128]{1,0:T(8,128)S(1)}, u32[]{:S(2)}, u32[]{:S(2)}) collective-permute-start(f32[112,128]{1,0:T(8,128)S(1)} %get-tuple-element.23), channel_id=1, source_target_pairs={{0,1},{2,3},{4,5},{6,7},{8,9},{10,11},{12,13},{14,15},{1,0},{3,2},... | collective-permute-start | bytes 172040 | tf_op jit(solution)/shard_map/ppermute | solution.py:407
  18.3 0.5 shard_map.67
  18.8 0.0 collective-permute-done.2.side_two
  18.9 0.3 collective-permute-done.3.side_one
  19.2 1.8 %shard_map.70 = (f32[96,1024]{1,0:T(8,128)S(1)}, f32[64,128]{1,0:T(8,128)S(1)}) custom-call(f32[32,8,128]{2,1,0:T(8,128)S(1)} %copy-done, f32[32,8,128]{2,1,0:T(8,128)S(1)} %copy-done.1, f32[8,128]{1,0:T(8,128)S(1)} %copy-done.2, f32[8,32,128]{2,1,0:T(8,128)S(1)} %get-tuple-element.16.inner_x, f32[8,32,128]{2,1,0:T(8,128)S(1)} %get-tuple-element.17.inner_p, ...), custom_call_target="tpu_custom_call" | custom-call | tf_op jit(solution)/shard_map/pallas_call | solution.py:392
  21.0 14.4 %all_to_all.23 = f32[16,4,128]{2,1,0:T(4,128)S(1)} all-to-all(f32[16,4,128]{2,1,0:T(4,128)S(1)} %bitcast.5), channel_id=1, replica_groups=mesh['gx'=32,'gy'=16] {'gy'}, dimensions={0} | all-to-all | bytes 65536 | tf_op jit(solution)/shard_map/all_to_all | solution.py:411
  35.4 21.6 %all_to_all.24 = f32[32,4,128]{2,1,0:T(4,128)S(1)} all-to-all(f32[32,4,128]{2,1,0:T(4,128)S(1)} %tile.4), channel_id=1, replica_groups=mesh['gx'=32,'gy'=16] {'gx'}, dimensions={0} | all-to-all | bytes 131072 | tf_op jit(solution)/shard_map/all_to_all | solution.py:411
  57.1 0.0 copy-start.3
  57.2 11.7 %all_to_all.25 = f32[16,4,128]{2,1,0:T(4,128)S(1)} all-to-all(f32[16,4,128]{2,1,0:T(4,128)S(1)} %tile.5), channel_id=1, replica_groups=mesh['gx'=32,'gy'=16] {'gy'}, dimensions={0} | all-to-all | bytes 65536 | tf_op jit(solution)/shard_map/all_to_all | solution.py:411
  68.9 0.0 copy-done.3
  68.9 5.0 %shard_map.71 = (f32[32,8,128]{2,1,0:T(8,128)}, f32[32,8,128]{2,1,0:T(8,128)}, f32[1,32]{1,0:T(1,128)}) custom-call(f32[64,128]{1,0:T(8,128)S(1)} %bitcast.4, s32[32,96]{1,0:T(8,128)S(1)} %bitcast.6, f32[96,1024]{1,0:T(8,128)S(1)} %get-tuple-element.25.refs_2_), custom_call_target="tpu_custom_call" | custom-call | tf_op jit(solution)/shard_map/pallas_call | solution.py:392
  (4 shorter events, 0.1 us)
Async XLA Ops:
  0.6 9.8 %copy-start.1 = (f32[32,8,128]{2,1,0:T(8,128)S(1)}, f32[32,8,128]{2,1,0:T(8,128)}, u32[]{:S(2)}) copy-start(f32[32,8,128]{2,1,0:T(8,128)} %search.5) | copy-start | bytes 393220
  0.6 9.8 %copy-start = (f32[32,8,128]{2,1,0:T(8,128)S(1)}, f32[32,8,128]{2,1,0:T(8,128)}, u32[]{:S(2)}) copy-start(f32[32,8,128]{2,1,0:T(8,128)} %basis.5) | copy-start | bytes 393220
  0.7 9.7 %copy-start.2 = (f32[8,128]{1,0:T(8,128)S(1)}, f32[8,128]{1,0:T(8,128)}, u32[]{:S(2)}) copy-start(f32[8,128]{1,0:T(8,128)} %cond.5) | copy-start | bytes 12292
  1.8 7.1 %collective-permute-start = (f32[104,128]{1,0:T(8,128)S(1)}, f32[104,128]{1,0:T(8,128)S(1)}, u32[]{:S(2)}, u32[]{:S(2)}) collective-permute-start(f32[104,128]{1,0:T(8,128)S(1)} %get-tuple-element.18), channel_id=1, source_target_pairs={{16,32},{48,64},{80,96},{112,128},{144,160},{176,192},{208,224},{2... | collective-permute-start | bytes 159752 | tf_op jit(solution)/shard_map/ppermute | solution.py:407
  2.5 7.9 %collective-permute-start.1 = (f32[104,128]{1,0:T(8,128)S(1)}, f32[104,128]{1,0:T(8,128)S(1)}, u32[]{:S(2)}, u32[]{:S(2)}) collective-permute-start(f32[104,128]{1,0:T(8,128)S(1)} %get-tuple-element.19), channel_id=1, source_target_pairs={{0,16},{32,48},{64,80},{96,112},{128,144},{160,176},{192,208},{224... | collective-permute-start | bytes 159752 | tf_op jit(solution)/shard_map/ppermute | solution.py:407
  10.8 8.1 %collective-permute-start.2 = (f32[112,128]{1,0:T(8,128)S(1)}, f32[112,128]{1,0:T(8,128)S(1)}, u32[]{:S(2)}, u32[]{:S(2)}) collective-permute-start(f32[112,128]{1,0:T(8,128)S(1)} %get-tuple-element.22), channel_id=1, source_target_pairs={{1,2},{3,4},{5,6},{7,8},{9,10},{11,12},{13,14},{2,1},{4,3},{6,5},{... | collective-permute-start | bytes 172040 | tf_op jit(solution)/shard_map/ppermute | solution.py:407
  15.7 3.5 %collective-permute-start.3 = (f32[112,128]{1,0:T(8,128)S(1)}, f32[112,128]{1,0:T(8,128)S(1)}, u32[]{:S(2)}, u32[]{:S(2)}) collective-permute-start(f32[112,128]{1,0:T(8,128)S(1)} %get-tuple-element.23), channel_id=1, source_target_pairs={{0,1},{2,3},{4,5},{6,7},{8,9},{10,11},{12,13},{14,15},{1,0},{3,2},... | collective-permute-start | bytes 172040 | tf_op jit(solution)/shard_map/ppermute | solution.py:407
  57.1 11.7 %copy-start.3 = (s32[96,32]{0,1:T(8,128)S(1)}, s32[96,32]{0,1:T(8,128)}, u32[]{:S(2)}) copy-start(s32[96,32]{0,1:T(8,128)} %param.7) | copy-start | bytes 36868
